TPU v7x, 512 devices: a whole 4x4x16 slice. The times are simulated.
512 devices in a mesh: ctx: 4 (over y), exp: 128 (over x, z, core).
Axes of the slice: x: 4, y: 4, z: 16, core: 2. Of those that a mesh axis runs over, the one named last changes fastest.
Arguments:
- queries: bfloat16 [256, 32, 2, 2048], P('exp', 'ctx'), may hold values from -20 to 20
- block_keys: bfloat16 [256, 32, 2, 256], P('exp', 'ctx'), may hold values from -6 to 6
- block_values: bfloat16 [256, 32, 2, 256], P('exp', 'ctx'), may hold values from -18 to 18
- cache_keys: bfloat16 [256, 512, 256], P('exp', 'ctx'), may hold values from -6 to 6
- cache_values: bfloat16 [256, 512, 256], P('exp', 'ctx'), may hold values from -18 to 18
- residual: bfloat16 [256, 32, 2, 2048], P('exp', 'ctx'), may hold values from -45 to 45
- out_weight: bfloat16 [2048, 2048], P('ctx'), may hold values from -0.125 to 0.125
- norm_gain: float32 [2048], replicated, may hold values from 0.1 to 1.9
- router: bfloat16 [2048, 128], P(None, 'exp'), may hold values from -0.5 to 0.5
- gate_weight: bfloat16 [128, 2048, 768], P('exp', None, 'ctx'), may hold values from -0.125 to 0.125
- up_weight: bfloat16 [128, 2048, 768], P('exp', None, 'ctx'), may hold values from -0.125 to 0.125
- down_weight: bfloat16 [128, 2048, 768], P('exp', None, 'ctx'), may hold values from -200 to 200
- expert_ids: int32 [256, 32, 2, 8], P('exp', 'ctx'), may hold values from 0 to 127, as said below
Outputs:
- block_output: bfloat16 [256, 32, 2, 2048], P('exp', 'ctx')
Inputs may be any that keep to these rules, and one draw needn't show every extreme that they name: `expert_ids`: each row names 8 different experts. Among the 32 rows of rollouts j * 2 to (j + 1) * 2 - 1 at positions m * 8 to (m + 1) * 8 - 1 (both steps), no expert is named by more than 4 rows, and some expert is named by exactly 4 of them.
All inputs are finite; a program needn't handle non-finite values.
Results may differ from a plain program's by a relative error of at most 0.029.
Values may be sent and summed in bfloat16 or wider, within the bound.
A program may use at most 64 MiB of HBM per device.

v0:
```python
import jax
import jax.numpy as jnp
from jax import lax
from jax.sharding import PartitionSpec as P

D = 2048
HEADS = 16
KV_HEADS = 2
HEAD_DIM = 128
TOPK = 8
BLOCK = 32


def combined_all(shard, axis, combine):
    everything = jax.tree.map(lambda part: lax.all_gather(part, axis), shard)
    initial = jax.tree.map(lambda part: part[0], everything)

    def step(k, so_far):
        return combine(so_far, jax.tree.map(lambda part: part[k], everything))

    return lax.fori_loop(1, lax.axis_size(axis), step, initial)


def round_trip(values):
    return lax.optimization_barrier(values.astype(jnp.bfloat16)).astype(jnp.float32)


def expert_part(tokens_in, gate_piece, up_piece, down_piece):
    gate_pre = jnp.dot(tokens_in, gate_piece, preferred_element_type=jnp.float32)
    up_pre = jnp.dot(tokens_in, up_piece, preferred_element_type=jnp.float32)
    activated = (jax.nn.silu(gate_pre) * up_pre).astype(jnp.bfloat16)
    partial_out = lax.dot_general(
        activated, down_piece, (((1,), (1,)), ((), ())), preferred_element_type=jnp.float32
    )
    return round_trip(partial_out)


def per_device(
    queries,
    block_keys,
    block_values,
    cache_keys,
    cache_values,
    residual,
    out_weight,
    norm_gain,
    router,
    gate_weight,
    up_weight,
    down_weight,
    expert_ids,
):
    ctx_count = lax.axis_size("ctx")
    ctx_index = lax.axis_index("ctx")
    experts = lax.axis_size("exp")
    roll_dev, pos_dev, step_count, query_width = queries.shape
    group_size = HEADS // KV_HEADS
    heads_here = HEADS // ctx_count
    score_scale = HEAD_DIM ** (-0.5)
    all_queries = lax.all_gather(queries, "ctx", axis=1, tiled=True)
    query_grid = all_queries.reshape(roll_dev, BLOCK, step_count, KV_HEADS, group_size, HEAD_DIM)
    cache_kgrid = cache_keys.reshape(roll_dev, -1, KV_HEADS, HEAD_DIM)
    cache_vgrid = cache_values.reshape(roll_dev, -1, KV_HEADS, HEAD_DIM)
    block_kgrid = block_keys.reshape(roll_dev, pos_dev, step_count, KV_HEADS, HEAD_DIM)
    block_vgrid = block_values.reshape(roll_dev, pos_dev, step_count, KV_HEADS, HEAD_DIM)
    far_scores = (
        jnp.einsum(
            "rpsgih,rjgh->prsgij", query_grid, cache_kgrid, preferred_element_type=jnp.float32
        )
        * score_scale
    )
    near_scores = (
        jnp.einsum(
            "rpsgih,rqsgh->prsgiq", query_grid, block_kgrid, preferred_element_type=jnp.float32
        )
        * score_scale
    )
    row_top = jnp.maximum(far_scores.max(-1), near_scores.max(-1))
    far_exp = jnp.exp(far_scores - row_top[..., None])
    near_exp = jnp.exp(near_scores - row_top[..., None])
    row_total = far_exp.sum(-1) + near_exp.sum(-1)
    weighted = jnp.einsum(
        "prsgij,rjgh->prsgih",
        far_exp.astype(jnp.bfloat16),
        cache_vgrid,
        preferred_element_type=jnp.float32,
    )
    weighted = weighted + jnp.einsum(
        "prsgiq,rqsgh->prsgih",
        near_exp.astype(jnp.bfloat16),
        block_vgrid,
        preferred_element_type=jnp.float32,
    )
    head_shape = (BLOCK, roll_dev, step_count, HEADS)
    row_top = row_top.reshape(head_shape)
    row_total = row_total.reshape(head_shape)
    weighted = weighted.reshape(head_shape + (HEAD_DIM,))

    def combine(first_part, second_part):
        new_top = jnp.maximum(first_part[0], second_part[0])
        first_scale = jnp.exp(first_part[0] - new_top)
        second_scale = jnp.exp(second_part[0] - new_top)
        return (
            new_top,
            first_part[1] * first_scale + second_part[1] * second_scale,
            first_part[2] * first_scale[..., None] + second_part[2] * second_scale[..., None],
        )

    merged_top, merged_total, merged_sum = combined_all(
        (row_top, row_total, weighted), "ctx", combine
    )
    own_total = lax.dynamic_slice_in_dim(merged_total, ctx_index * heads_here, heads_here, 3)
    own_sum = lax.dynamic_slice_in_dim(merged_sum, ctx_index * heads_here, heads_here, 3)
    attended = (
        (own_sum / own_total[..., None])
        .reshape(BLOCK, roll_dev, step_count, heads_here * HEAD_DIM)
        .astype(jnp.bfloat16)
    )
    head_sum = lax.psum_scatter(
        jnp.einsum(
            "prsk,kd->prsd", attended, out_weight, preferred_element_type=jnp.float32
        ).astype(jnp.bfloat16),
        "ctx",
        scatter_dimension=0,
        tiled=True,
    ).astype(jnp.float32)
    hidden = residual.astype(jnp.float32) + head_sum.transpose(1, 0, 2, 3)
    normed = (
        hidden * lax.rsqrt(jnp.mean(hidden * hidden, -1, keepdims=True) + 1e-06) * norm_gain
    ).astype(jnp.bfloat16)
    token_total = roll_dev * pos_dev * step_count
    token_rows = normed.reshape(token_total, D)
    flat_ids = expert_ids.reshape(-1)
    assigned = flat_ids.shape[0]
    capacity = min(token_total, max(2, 2 * assigned // experts))
    expert_hits = (flat_ids[:, None] == jnp.arange(experts, dtype=jnp.int32)[None, :]).astype(
        jnp.int32
    )
    earlier = jnp.cumsum(expert_hits, 0) - expert_hits
    rank_within = jnp.sum(earlier * expert_hits, 1)
    slot_ids = flat_ids * capacity + rank_within
    placement_map = (
        slot_ids[:, None] == jnp.arange(experts * capacity, dtype=jnp.int32)[None, :]
    ).astype(jnp.bfloat16)
    token_map = placement_map.reshape(token_total, TOPK, experts * capacity).sum(1)
    outgoing = lax.dot_general(
        token_map, token_rows, (((0,), (0,)), ((), ())), preferred_element_type=jnp.float32
    )
    outgoing = outgoing.astype(jnp.bfloat16).reshape(experts, capacity, D)
    full_gate, full_up, full_down = (
        lax.all_gather(gate_weight, "ctx", axis=2, tiled=True),
        lax.all_gather(up_weight, "ctx", axis=2, tiled=True),
        lax.all_gather(down_weight, "ctx", axis=2, tiled=True),
    )
    quarter = gate_weight.shape[2]
    arrived = lax.all_to_all(outgoing, "exp", split_axis=0, concat_axis=0, tiled=True)
    sources, slots_here, feature_width = arrived.shape
    flat_rows = arrived.reshape(sources * slots_here, feature_width)
    combined = jnp.zeros((flat_rows.shape[0], D), jnp.float32)
    for quarter_index in range(ctx_count):
        lower_edge = quarter_index * quarter
        combined = combined + expert_part(
            flat_rows,
            full_gate[0, :, lower_edge : lower_edge + quarter],
            full_up[0, :, lower_edge : lower_edge + quarter],
            full_down[0, :, lower_edge : lower_edge + quarter],
        )
    expert_out = combined.astype(jnp.bfloat16).reshape(sources, slots_here, feature_width)
    router_scores = (
        jnp.dot(flat_rows, router, preferred_element_type=jnp.float32)
        .astype(jnp.bfloat16)
        .reshape(sources, slots_here)
    )
    back_rows = lax.all_to_all(expert_out, "exp", split_axis=0, concat_axis=0, tiled=True)
    back_scores = lax.all_to_all(router_scores, "exp", split_axis=0, concat_axis=0, tiled=True)
    chosen_rows = (
        jnp.take(back_rows.reshape(experts * capacity, D), slot_ids, axis=0)
        .astype(jnp.float32)
        .reshape(token_total, TOPK, D)
    )
    chosen_scores = (
        jnp.take(back_scores.reshape(-1), slot_ids).astype(jnp.float32).reshape(token_total, TOPK)
    )
    gate_values = jnp.exp(chosen_scores - jnp.max(chosen_scores, -1, keepdims=True))
    mix_weight = gate_values / jnp.sum(gate_values, -1, keepdims=True)
    expert_mix = jnp.sum(mix_weight[..., None] * chosen_rows, 1)
    block_output = (hidden.reshape(token_total, D) + expert_mix).astype(jnp.bfloat16)
    return block_output.reshape(residual.shape)


def solution(mesh):
    in_specs = (
        P("exp", "ctx", None, None),
        P("exp", "ctx", None, None),
        P("exp", "ctx", None, None),
        P("exp", "ctx", None),
        P("exp", "ctx", None),
        P("exp", "ctx", None, None),
        P("ctx", None),
        P(),
        P(None, "exp"),
        P("exp", None, "ctx"),
        P("exp", None, "ctx"),
        P("exp", None, "ctx"),
        P("exp", "ctx", None, None),
    )
    out_specs = P("exp", "ctx", None, None)
    return jax.shard_map(
        per_device, mesh=mesh, in_specs=in_specs, out_specs=out_specs, check_vma=False
    )
```

profile of v0, /device:TPU:1, one launch (start us, length us, event | category | flops | bytes accessed | tf_op | source)
XLA Modules:
  0.0 453.8 jit_solution(12894963735138079480)
XLA Ops:
  6.5 0.9 reshape.241
  8.2 0.9 reshape.239
  9.1 0.9 reshape.242
  10.1 11.5 %all_gather.21 = bf16[2,32,2,2048]{3,2,1,0:T(2,128)(2,1)S(1)} all-gather(bf16[2,8,2,2048]{3,2,1,0:T(2,128)(2,1)} %param.15), channel_id=1, replica_groups=mesh['ctx'=4,'exp'=128] {'ctx'}, dimensions={1}, use_global_device_ids=true | all-gather | bytes 655360 | tf_op jit(solution)/shard_map/all_gather | solution.py:60
  21.8 0.8 fusion.70
  25.1 1.1 copy.243
  26.3 9.1 %all_gather.23 = f32[4,32,2,2,16]{1,4,3,2,0:T(8,128)S(1)} all-gather(f32[1,32,2,2,16]{1,4,3,2,0:T(8,128)S(1)} %copy_bitcast_fusion.1), channel_id=1, replica_groups=mesh['ctx'=4,'exp'=128] {'ctx'}, dimensions={0}, use_global_device_ids=true | all-gather | bytes 40960 | tf_op jit(solution)/shard_map/all_gather | solution.py:15
  35.4 9.3 %all_gather.22 = f32[4,32,2,2,16]{1,4,3,2,0:T(8,128)S(1)} all-gather(f32[1,32,2,2,16]{1,4,3,2,0:T(8,128)S(1)} %bitcast.144), channel_id=1, replica_groups=mesh['ctx'=4,'exp'=128] {'ctx'}, dimensions={0}, use_global_device_ids=true | all-gather | bytes 40960 | tf_op jit(solution)/shard_map/all_gather | solution.py:15
  45.3 44.5 %all-gather.5.cloned.1.call-done = f32[4,32,2,2,16,128]{5,4,3,2,1,0:T(8,128)} async-done(((f32[1,32,2,2,16,128]{5,4,3,2,1,0:T(8,128)}), f32[4,32,2,2,16,128]{5,4,3,2,1,0:T(8,128)}) %all-gather.5.cloned.1.call-update) | async-done | bytes 4194320 | tf_op jit(solution)/shard_map/all_gather | solution.py:15
  89.8 1.3 slice_bitcast_fusion
  91.1 8.8 %while.19 = (s32[]{:T(128)}, f32[32,2,2,16]{0,3,2,1:T(8,128)S(1)}, f32[32,2,2,16]{0,3,2,1:T(8,128)S(1)}, f32[32,2,2,16,128]{4,3,2,1,0:T(8,128)S(1)}, f32[4,32,2,...) while((s32[]{:T(128)}, f32[32,2,2,16]{0,3,2,1:T(8,128)S(1)}, ...), condition=%wide.region_5.0_spmd, body=%wide.region_4.0_spmd.sunk | while | flops 798725 | bytes 3260559 | solution.py:21
  91.2 0.8 fusion.87
  92.2 1.9 fusion.88
  94.1 0.8 fusion.87
  95.1 1.9 fusion.88
  97.0 0.8 fusion.87
  98.0 1.9 fusion.88
  101.4 1.2 reshape.277
  105.1 25.4 %reduce-scatter.4.cloned.1.call-done = bf16[8,8192]{1,0:T(8,128)(2,1)} async-done(((bf16[32,8192]{1,0:T(8,128)(2,1)}), bf16[8,8192]{1,0:T(8,128)(2,1)}) %reduce-scatter.4.cloned.1.call-update) | async-done | bytes 131088
  130.5 1.1 multiply_reduce_fusion.1
  131.6 1.0 multiply_convert_fusion
  132.8 2.1 convolution_convert_fusion.4
  134.8 4.1 reshape.246
  139.0 18.8 %all-to-all-start = ((bf16[128,4,2048]{2,1,0:T(4,128)(2,1)}), bf16[128,4,2048]{2,1,0:T(4,128)(2,1)}, u32[]{:S(2)}, u32[]{:S(2)}) async-start(bf16[128,4,2048]{2,1,0:T(4,128)(2,1)} %reshape.246), calls=%async_computation | async-start | bytes 4194304 | tf_op jit(solution)/shard_map/all_to_all | solution.py:156
  158.4 98.2 %all-to-all-done = bf16[128,4,2048]{2,1,0:T(4,128)(2,1)} async-done(((bf16[128,4,2048]{2,1,0:T(4,128)(2,1)}), bf16[128,4,2048]{2,1,0:T(4,128)(2,1)}, u32[]{:S(2)}, u32[]{:S(2)}) %all-to-all-start) | async-done | bytes 2097184 | tf_op jit(solution)/shard_map/all_to_all | solution.py:156
  256.5 4.0 reshape.247
  260.5 2.2 fusion.71
  262.7 0.8 all_to_all.16
  263.5 8.7 %all-to-all-start.1 = ((bf16[128,1,4]{2,1,0:T(2,128)(2,1)}), bf16[128,1,4]{2,1,0:T(2,128)(2,1)S(1)}, u32[]{:S(2)}, u32[]{:S(2)}) async-start(bf16[128,1,4]{2,1,0:T(2,128)(2,1)} %all_to_all.16), calls=%async_computation.1 | async-start | bytes 131072 | tf_op jit(solution)/shard_map/all_to_all | solution.py:175
  272.3 2.7 fusion.16
  275.0 5.4 %all-gather.11.cloned.1.call-done = bf16[1,2048,768]{1,2,0:T(8,128)(2,1)} async-done(((bf16[1,2048,192]{1,2,0:T(8,128)(2,1)}), bf16[1,2048,768]{1,2,0:T(8,128)(2,1)}) %all-gather.11.cloned.1.call-update) | async-done | bytes 3145744 | tf_op jit(solution)/shard_map/all_gather | solution.py:153
  280.3 5.0 %convolution_convert_fusion.3 = bf16[512,2048]{1,0:T(8,128)(2,1)} fusion(bf16[512,2048]{1,0:T(8,128)(2,1)} %reshape.247, bf16[1,2048,768]{1,2,0:T(8,128)(2,1)} %all-gather.11.cloned.1.call-done, bf16[1,2048,768]{1,2,0:T(8,128)(2,1)} %all-gather.9.cloned.1.call-done, f32[512,192]{0,1:T(8,128)S(1)} %fusion.16), kind=kOutput, calls=%fused_computation.14 | convolution fusion | flops 806944768 | bytes 6160384 | tf_op jit(solution)/shard_map/dot_general | solution.py:32
  285.3 2.6 fusion.15
  288.0 4.9 %convolution_convert_fusion.2 = bf16[512,2048]{1,0:T(8,128)(2,1)} fusion(bf16[512,2048]{1,0:T(8,128)(2,1)} %reshape.247, bf16[1,2048,768]{1,2,0:T(8,128)(2,1)} %all-gather.11.cloned.1.call-done, bf16[1,2048,768]{1,2,0:T(8,128)(2,1)} %all-gather.9.cloned.1.call-done, f32[512,192]{0,1:T(8,128)S(1)} %fusion.15), kind=kOutput, calls=%fused_computation.13 | convolution fusion | flops 806944768 | bytes 6160384 | tf_op jit(solution)/shard_map/dot_general | solution.py:32
  292.9 2.6 fusion.13
  295.5 4.9 %convolution_convert_fusion = bf16[512,2048]{1,0:T(8,128)(2,1)} fusion(bf16[512,2048]{1,0:T(8,128)(2,1)} %reshape.247, bf16[1,2048,768]{1,2,0:T(8,128)(2,1)} %all-gather.11.cloned.1.call-done, bf16[1,2048,768]{1,2,0:T(8,128)(2,1)} %all-gather.9.cloned.1.call-done, f32[512,192]{0,1:T(8,128)S(1)} %fusion.13), kind=kOutput, calls=%fused_computation.11 | convolution fusion | flops 806944768 | bytes 6160384 | tf_op jit(solution)/shard_map/dot_general | solution.py:32
  300.4 2.6 fusion.14
  303.0 5.0 %convolution_convert_fusion.1 = bf16[512,2048]{1,0:T(8,128)(2,1)} fusion(bf16[512,2048]{1,0:T(8,128)(2,1)} %reshape.247, bf16[1,2048,768]{1,2,0:T(8,128)(2,1)} %all-gather.11.cloned.1.call-done, bf16[1,2048,768]{1,2,0:T(8,128)(2,1)} %all-gather.9.cloned.1.call-done, f32[512,192]{0,1:T(8,128)S(1)} %fusion.14), kind=kOutput, calls=%fused_computation.12 | convolution fusion | flops 806944768 | bytes 6160384 | tf_op jit(solution)/shard_map/dot_general | solution.py:32
  308.0 6.8 %add_convert_fusion = bf16[512,2048]{1,0:T(8,128)(2,1)} fusion(bf16[512,2048]{1,0:T(8,128)(2,1)} %convolution_convert_fusion, bf16[512,2048]{1,0:T(8,128)(2,1)} %convolution_convert_fusion.1, bf16[512,2048]{1,0:T(8,128)(2,1)} %convolution_convert_fusion.2, bf16[512,2048]{1,0:T(8,128)(2,1)} %convolution_convert_fusion.3), kind=kLoop, calls=%fused_computation.10 | loop fusion | flops 8388608 | bytes 10485760 | tf_op jit(solution)/shard_map/convert_element_type | solution.py:168
  314.8 4.1 reshape.250
  318.9 17.1 %all-to-all-start.2 = ((bf16[128,4,2048]{2,1,0:T(4,128)(2,1)}), bf16[128,4,2048]{2,1,0:T(4,128)(2,1)}, u32[]{:S(2)}, u32[]{:S(2)}) async-start(bf16[128,4,2048]{2,1,0:T(4,128)(2,1)} %reshape.250), calls=%async_computation.2 | async-start | bytes 4194304 | tf_op jit(solution)/shard_map/all_to_all | solution.py:174
  336.4 1.9 gather_fusion
  338.8 95.9 %all-to-all-done.2 = bf16[128,4,2048]{2,1,0:T(4,128)(2,1)} async-done(((bf16[128,4,2048]{2,1,0:T(4,128)(2,1)}), bf16[128,4,2048]{2,1,0:T(4,128)(2,1)}, u32[]{:S(2)}, u32[]{:S(2)}) %all-to-all-start.2) | async-done | bytes 2097184 | tf_op jit(solution)/shard_map/all_to_all | solution.py:174
  434.7 4.0 reshape.251
  438.7 4.3 gather_fusion.1
  443.0 2.2 multiply_reduce_fusion
  445.2 1.1 reduce_sum.81
  446.5 0.8 copy.186
  (81 shorter events, 10.4 us)
Async XLA Ops:
  6.5 93.8 %copy-start = (bf16[512,2048]{1,0:T(8,128)(2,1)S(1)}, bf16[512,2048]{1,0:T(8,128)(2,1)}, u32[]{:S(2)}) copy-start(bf16[512,2048]{1,0:T(8,128)(2,1)} %param.21) | copy-start | bytes 6291460
  6.5 83.3 %all-gather.5.cloned.1.call-start = ((), (), s32[]{:S(2)}) async-start(), calls=%async_computation.4 | async-start | bytes 5242880 | tf_op jit(solution)/shard_map/all_gather | solution.py:15
  26.2 104.3 %reduce-scatter.4.cloned.1.call-start = ((), (), s32[]{:S(2)}) async-start(), calls=%async_computation.8 | async-start | bytes 655360
  44.7 0.7 copy-start.3
  100.8 3.1 copy-start.4
  101.4 29.1 %copy-start.1 = (bf16[2,8,2,2048]{3,2,1,0:T(2,128)(2,1)S(1)}, bf16[2,8,2,2048]{3,2,1,0:T(2,128)(2,1)}, u32[]{:S(2)}) copy-start(bf16[2,8,2,2048]{3,2,1,0:T(2,128)(2,1)} %param.20) | copy-start | bytes 393220
  101.4 30.2 %copy-start.6 = (f32[2048]{0:T(1024)S(1)}, f32[2048]{0:T(1024)}, u32[]{:S(2)}) copy-start(f32[2048]{0:T(1024)} %param.22) | copy-start | bytes 24580
  102.6 169.6 %all-gather.7.cloned.1.call-start = ((), (), s32[]{:S(2)}) async-start(), calls=%async_computation.5 | async-start | bytes 3932160 | tf_op jit(solution)/shard_map/all_gather | solution.py:151
  103.4 171.6 %all-gather.9.cloned.1.call-start = ((), (), s32[]{:S(2)}) async-start(), calls=%async_computation.6 | async-start | bytes 3932160 | tf_op jit(solution)/shard_map/all_gather | solution.py:152
  139.0 117.5 %all-to-all-start = ((bf16[128,4,2048]{2,1,0:T(4,128)(2,1)}), bf16[128,4,2048]{2,1,0:T(4,128)(2,1)}, u32[]{:S(2)}, u32[]{:S(2)}) async-start(bf16[128,4,2048]{2,1,0:T(4,128)(2,1)} %reshape.246), calls=%async_computation | async-start | bytes 4194304 | tf_op jit(solution)/shard_map/all_to_all | solution.py:156
  157.7 122.6 %all-gather.11.cloned.1.call-start = ((), (), s32[]{:S(2)}) async-start(), calls=%async_computation.7 | async-start | bytes 3932160 | tf_op jit(solution)/shard_map/all_gather | solution.py:153
  158.3 102.1 %copy-start.5 = (bf16[2048,1]{0,1:T(2,128)(2,1)S(1)}, bf16[2048,1]{0,1:T(2,128)(2,1)}, u32[]{:S(2)}) copy-start(bf16[2048,1]{0,1:T(2,128)(2,1)} %param.23) | copy-start | bytes 12292
  263.5 55.4 %all-to-all-start.1 = ((bf16[128,1,4]{2,1,0:T(2,128)(2,1)}), bf16[128,1,4]{2,1,0:T(2,128)(2,1)S(1)}, u32[]{:S(2)}, u32[]{:S(2)}) async-start(bf16[128,1,4]{2,1,0:T(2,128)(2,1)} %all_to_all.16), calls=%async_computation.1 | async-start | bytes 131072 | tf_op jit(solution)/shard_map/all_to_all | solution.py:175
  318.9 115.9 %all-to-all-start.2 = ((bf16[128,4,2048]{2,1,0:T(4,128)(2,1)}), bf16[128,4,2048]{2,1,0:T(4,128)(2,1)}, u32[]{:S(2)}, u32[]{:S(2)}) async-start(bf16[128,4,2048]{2,1,0:T(4,128)(2,1)} %reshape.250), calls=%async_computation.2 | async-start | bytes 4194304 | tf_op jit(solution)/shard_map/all_to_all | solution.py:174
  438.7 7.6 %copy-start.2 = (bf16[8,8192]{1,0:T(8,128)(2,1)S(1)}, bf16[8,8192]{1,0:T(8,128)(2,1)}, u32[]{:S(2)}) copy-start(bf16[8,8192]{1,0:T(8,128)(2,1)} %reduce-scatter.4.cloned.1.call-done) | copy-start | bytes 393220
Sparse Core Ops, SparseCore 0:
  26.3 63.4 all-gather.4
  102.8 27.6 reduce-scatter.3
  132.6 48.7 all-gather.6
  183.3 47.4 all-gather.8
  232.8 47.4 all-gather.10
where the time goes:
time: 455 us; the launch traced here: 454 us
  waiting for transfers between devices  271 us (60%)
  starting transfers between devices  44.7 us (10%)
  matrix products  37 us (8%)
  local copies, waits for them, and re-layouts  35.8 us (8%)
  blocking collectives  29.9 us (7%)
  other arithmetic  21.6 us (5%)
  between operations  13.5 us (3%)
    all_to_all x1, waiting for transfers between devices, per_device(): lax.all_to_all(outgoing, 'exp', split_axis=0, concat_axis=0, tiled=True)  98.2 us
    all_to_all x1, waiting for transfers between devices, per_device(): lax.all_to_all(expert_out, 'exp', split_axis=0, concat_axis=0, tiled=True)  95.9 us
    all_gather x1, waiting for transfers between devices, combined_all(): everything = jax.tree.map(lambda part: lax.all_gather(part, axis), shard)  44.5 us
    unnamed x6, waiting for transfers between devices  27.2 us
    dot_general x4, matrix products, expert_part(): lax.dot_general(activated, down_piece, (((1,), (1,)), ((), ())), preferre...  19.8 us
    all_to_all x1, starting transfers between devices, per_device(): lax.all_to_all(outgoing, 'exp', split_axis=0, concat_axis=0, tiled=True)  18.8 us
    all_gather x2, blocking collectives, combined_all(): everything = jax.tree.map(lambda part: lax.all_gather(part, axis), shard)  18.4 us
    all_to_all x1, starting transfers between devices, per_device(): lax.all_to_all(expert_out, 'exp', split_axis=0, concat_axis=0, tiled=True)  17.1 us
  transfers between devices with their start and end apart: 8, of which 5 were waited for; matrix products, arithmetic and copies ran while one was open for 13% of the time, Pallas kernels for 0%

commit v1 on v0

v1 whole, which is shorter than its diff:
```python
import jax
import jax.numpy as jnp
from jax import lax
from jax.experimental import pallas as pl
from jax.experimental.pallas import tpu as pltpu
from jax.sharding import PartitionSpec as P

D = 2048
HEAD_DIM = 128
TOPK = 8


MESH = pl.DeviceIdType.MESH
BF = jnp.bfloat16
F32 = jnp.float32
NT = (((1,), (1,)), ((), ()))
TOK = 32
ZN = 16


def slot_of(direction, distance):
    if distance == 8:
        return 15
    return 2 * distance - 1 + direction


def layer_kernel(
    queries, block_keys, block_values, cache_keys, cache_values, residual, out_weight,
    gain, router, ids, gate, up, down, out,
    q_all, k_all, v_all, bk_all, bv_all, att, ow, psend, precv, hid, rg, rgf, rfull,
    tok, met, swt, sendx, rx, acc, ysend, ry, part, rss, rsr, wb,
    ex_s, ex_r, own_l, p_s, p_r, rz_s, rz_r, rp_s, rp_r,
    tok_s, tok_r, met_s, met_r, x_s, x_r, y_s, y_r, rs_s, rs_r,
    w_s, w_r, v_s, v_r, loc,
):
    y = lax.axis_index("ctx")
    e = lax.axis_index("exp")
    core = lax.rem(e, 2)
    z = lax.rem(e // 2, ZN)
    x = e // 32
    me8 = x * 2 + core

    def at_z(other):
        return (y, x * 32 + other * 2 + core)

    def at_peer(p):
        return (y, (p // 2) * 32 + z * 2 + lax.rem(p, 2))

    z_next = (at_z(lax.rem(z + 1, ZN)), at_z(lax.rem(z + ZN - 1, ZN)))
    def at_y(d):
        return (lax.rem(y + d, 4), e)

    y_next = (at_y(1), at_y(3))

    barrier = pltpu.get_barrier_semaphore()
    for target in z_next + y_next + (at_y(2),):
        pl.semaphore_signal(barrier, inc=1, device_id=target, device_id_type=MESH)
    for d in range(1, 8):
        pl.semaphore_signal(
            barrier, inc=1, device_id=at_peer(lax.rem(me8 + d, 8)), device_id_type=MESH
        )

    weights = (gate, up, down)
    own_copies = []
    for a in range(3):
        copy = pltpu.make_async_copy(weights[a], wb.at[0, pl.ds(192 * a, 192)], loc.at[a])
        copy.start()
        own_copies.append(copy)

    def columns(index, width):
        return pl.ds(pl.multiple_of(index * width, width), width)

    def shares(owner):
        group = owner // 2
        return (
            queries.at[:, columns(owner, 512)],
            cache_keys.at[:, columns(group, 128)],
            cache_values.at[:, columns(group, 128)],
            block_keys.at[:, columns(group, 128)],
            block_values.at[:, columns(group, 128)],
        )

    gathered = (q_all, k_all, v_all, bk_all, bv_all)
    for a, share in enumerate(shares(y)):
        copy = pltpu.make_async_copy(share, gathered[a].at[y], own_l.at[a])
        copy.start()
        own_copies.append(copy)
    copy = pltpu.make_async_copy(out_weight, ow, own_l.at[5])
    copy.start()
    own_copies.append(copy)
    rg[x, z, core] = router[...]

    pl.semaphore_wait(barrier, 12)

    def exchange(d, a):
        owner = lax.rem(y + d, 4)
        return pltpu.make_async_remote_copy(
            src_ref=shares(owner)[a],
            dst_ref=gathered[a].at[y],
            send_sem=ex_s.at[d - 1, a],
            recv_sem=ex_r.at[d - 1, a],
            device_id=at_y(d),
            device_id_type=MESH,
        )

    def exchanged(d, a):
        source = lax.rem(y + 4 - d, 4)
        pltpu.make_async_remote_copy(
            src_ref=gathered[a].at[source],
            dst_ref=gathered[a].at[source],
            send_sem=ex_s.at[d - 1, a],
            recv_sem=ex_r.at[d - 1, a],
            device_id=at_y(d),
            device_id_type=MESH,
        ).wait_recv()

    for d in (2, 1, 3):
        for a in range(5):
            exchange(d, a).start()

    def ring_row(dr, k):
        held = lax.rem(z + (k - 1 if dr else ZN + 1 - k), ZN)
        return pltpu.make_async_remote_copy(
            src_ref=rg.at[x, held, core],
            dst_ref=rg.at[x, held, core],
            send_sem=rz_s.at[dr, k - 1],
            recv_sem=rz_r.at[dr, k - 1],
            device_id=z_next[dr],
            device_id_type=MESH,
        )

    def ring_row_landed(dr, k):
        held = lax.rem(z + (k if dr else ZN - k), ZN)
        pltpu.make_async_remote_copy(
            src_ref=rg.at[x, held, core],
            dst_ref=rg.at[x, held, core],
            send_sem=rz_s.at[dr, k - 1],
            recv_sem=rz_r.at[dr, k - 1],
            device_id=z_next[dr],
            device_id_type=MESH,
        ).wait_recv()

    def router_rows(d, landed_here):
        p = lax.rem(me8 + 8 - d, 8) if landed_here else me8
        return pltpu.make_async_remote_copy(
            src_ref=rg.at[p // 2, :, lax.rem(p, 2)],
            dst_ref=rg.at[p // 2, :, lax.rem(p, 2)],
            send_sem=rp_s.at[d - 1],
            recv_sem=rp_r.at[d - 1],
            device_id=at_peer(lax.rem(me8 + d, 8)),
            device_id_type=MESH,
        )

    w_copy, v_copy = {}, {}
    for dr in range(2):
        for a in range(3):
            for half in range(2):
                w_copy[dr, a, half] = pltpu.make_async_remote_copy(
                    src_ref=weights[a].at[pl.ds(96 * half, 96)],
                    dst_ref=wb.at[1 + dr, pl.ds(192 * a + 96 * half, 96)],
                    send_sem=w_s.at[dr, a, half],
                    recv_sem=w_r.at[dr, a, half],
                    device_id=y_next[dr],
                    device_id_type=MESH,
                )
            rows = pl.ds(192 * a + 96 * dr, 96)
            v_copy[dr, a] = pltpu.make_async_remote_copy(
                src_ref=wb.at[1 + dr, rows],
                dst_ref=wb.at[3, rows],
                send_sem=v_s.at[dr, a],
                recv_sem=v_r.at[dr, a],
                device_id=y_next[dr],
                device_id_type=MESH,
            )
    for a in range(2):
        for dr in range(2):
            w_copy[dr, a, dr].start()

    ring_row(0, 1).start()
    ring_row(1, 1).start()
    for k in range(1, 9):
        for dr in range(2):
            if k < 8 or dr == 0:
                ring_row_landed(dr, k)
                if k < 7 or (k == 7 and dr == 0):
                    ring_row(dr, k + 1).start()
    for d in range(1, 8):
        router_rows(d, False).start()

    for copy in own_copies:
        copy.wait()
    for d in range(1, 4):
        for a in range(5):
            exchanged(d, a)

    key_step = lax.rem(lax.broadcasted_iota(jnp.int32, (256, 64), 1), 2)
    row_step = lax.rem(lax.broadcasted_iota(jnp.int32, (256, 64), 0), 2)
    for r in range(2):
        near, far = slice(16 * r, 16 * r + 16), slice(128 * r, 128 * r + 128)
        q_rows = jnp.concatenate(
            [q_all[m, near, 128 * h : 128 * h + 128] for h in range(4) for m in range(4)], 0
        )
        far_scores = lax.dot_general(
            q_rows, k_all[:, far, :].reshape(512, 128), NT, preferred_element_type=F32
        )
        near_scores = lax.dot_general(
            q_rows, bk_all[:, near, :].reshape(64, 128), NT, preferred_element_type=F32
        )
        far_scores = far_scores * HEAD_DIM ** (-0.5)
        near_scores = jnp.where(
            key_step == row_step, near_scores * HEAD_DIM ** (-0.5), -3e38
        )
        row_top = jnp.maximum(
            jnp.max(far_scores, -1, keepdims=True), jnp.max(near_scores, -1, keepdims=True)
        )
        far_exp = jnp.exp(far_scores - row_top)
        near_exp = jnp.where(key_step == row_step, jnp.exp(near_scores - row_top), 0.0)
        total = jnp.sum(far_exp, -1, keepdims=True) + jnp.sum(near_exp, -1, keepdims=True)
        weighted = jnp.dot(
            far_exp.astype(BF), v_all[:, far, :].reshape(512, 128), preferred_element_type=F32
        ) + jnp.dot(
            near_exp.astype(BF), bv_all[:, near, :].reshape(64, 128), preferred_element_type=F32
        )
        attended = (weighted / total).astype(BF)
        for h in range(4):
            for m in range(4):
                att[m, near, 128 * h : 128 * h + 128] = attended[
                    64 * h + 16 * m : 64 * h + 16 * m + 16
                ]

    for c in range(4):
        cols = slice(512 * c, 512 * c + 512)
        projected = jnp.dot(
            att[...].reshape(128, 512), ow[:, cols], preferred_element_type=F32
        ).reshape(4, TOK, 512)
        part[0:4, :, cols] = projected
        psend[:, :, cols] = projected.astype(BF)

    p_copy = []
    for d in (2, 1, 3):
        p_copy.append(
            pltpu.make_async_remote_copy(
                src_ref=psend.at[lax.rem(y + d, 4)],
                dst_ref=precv.at[d - 1],
                send_sem=p_s.at[d - 1],
                recv_sem=p_r.at[d - 1],
                device_id=at_y(d),
                device_id_type=MESH,
            )
        )
        p_copy[-1].start()
    for dr in range(2):
        w_copy[dr, 2, dr].start()
    for a in range(3):
        for dr in range(2):
            w_copy[dr, a, 1 - dr].start()

    for d in range(1, 8):
        router_rows(d, True).wait_recv()
    rgf[...] = rg[...].reshape(2048, 128).astype(F32)
    for k in range(16):
        rfull[:, 128 * k : 128 * k + 128] = rgf[pl.ds(k, 128, stride=16), :].astype(BF)

    for copy in p_copy:
        copy.wait_recv()
    hidden = residual[...].astype(F32) + part[y]
    for d in range(3):
        hidden = hidden + precv[d].astype(F32)
    hid[...] = hidden
    scale = lax.rsqrt(jnp.mean(hidden * hidden, -1, keepdims=True) + 1e-06)
    normed = (hidden * scale * gain[...]).astype(BF)
    tok[0] = normed
    scores = lax.dot_general(rfull[...], normed, NT, preferred_element_type=F32)
    scores = scores.astype(BF).astype(F32)
    expert_row = lax.broadcasted_iota(jnp.int32, (128, TOK), 0)
    named = expert_row == ids[0:1, :]
    for k in range(1, 8):
        named = named | (expert_row == ids[k : k + 1, :])
    hits = jnp.where(named, 1.0, 0.0)
    top = jnp.max(jnp.where(named, scores, -3e38), 0, keepdims=True)
    grown = jnp.where(named, jnp.exp(jnp.minimum(scores - top, 0.0)), 0.0)
    mix = grown / jnp.sum(grown, 0, keepdims=True)
    before = lax.broadcasted_iota(jnp.int32, (TOK, TOK), 0) < lax.broadcasted_iota(
        jnp.int32, (TOK, TOK), 1
    )
    rank = jnp.dot(
        hits.astype(BF), jnp.where(before, 1.0, 0.0).astype(BF), preferred_element_type=F32
    )
    code = jnp.where(named, 2.0 * rank + mix, -1.0)
    for k in range(4):
        met[0, :, 32 * k : 32 * k + 32] = code[32 * k : 32 * k + 32, :]

    tok_copy, met_copy = {}, {}
    for dr in range(2):
        for k in range(1, 9):
            src = 0 if k == 1 else slot_of(dr, k - 1)
            dst = slot_of(dr, k)
            for half in range(2):
                if k == 8 and half != dr:
                    continue
                rows = pl.ds(16 * half, 16)
                tok_copy[dr, k, half] = pltpu.make_async_remote_copy(
                    src_ref=tok.at[src, rows],
                    dst_ref=tok.at[dst, rows],
                    send_sem=tok_s.at[dr, k - 1, half],
                    recv_sem=tok_r.at[dr, k - 1, half],
                    device_id=z_next[dr],
                    device_id_type=MESH,
                )
            if k < 8 or dr == 0:
                met_copy[dr, k] = pltpu.make_async_remote_copy(
                    src_ref=met.at[src],
                    dst_ref=met.at[dst],
                    send_sem=met_s.at[dr, k - 1],
                    recv_sem=met_r.at[dr, k - 1],
                    device_id=z_next[dr],
                    device_id_type=MESH,
                )

    for dr in range(2):
        met_copy[dr, 1].start()
        tok_copy[dr, 1, 0].start()
        tok_copy[dr, 1, 1].start()

    row = lax.broadcasted_iota(jnp.int32, (128, 128), 0)
    lane = lax.broadcasted_iota(jnp.int32, (128, 128), 1)
    row_x, row_c = row // 32, lax.rem(row // 16, 2)
    row_q, row_s = lax.rem(row // 4, 4), lax.rem(row, 4)
    lane_g = lane // 32

    def folded(values):
        total = values
        for k in range(1, 4):
            total = total + pltpu.roll(values, 32 * k, 1)
        return jnp.where(lane_g == row_q, total, 0.0)

    def x_copy(g, d):
        p = lax.rem(me8 + d, 8)
        return pltpu.make_async_remote_copy(
            src_ref=sendx.at[g, p],
            dst_ref=rx.at[g, me8],
            send_sem=x_s.at[g, d - 1],
            recv_sem=x_r.at[g, d - 1],
            device_id=at_peer(p),
            device_id_type=MESH,
        )

    def y_copy(g, d):
        p = lax.rem(me8 + d, 8)
        return pltpu.make_async_remote_copy(
            src_ref=ysend.at[g, p],
            dst_ref=ry.at[g, me8],
            send_sem=y_s.at[g, d - 1],
            recv_sem=y_r.at[g, d - 1],
            device_id=at_peer(p),
            device_id_type=MESH,
        )

    def landed(buffer, sems, g, d):
        p = lax.rem(me8 + 8 - d, 8)
        pltpu.make_async_remote_copy(
            src_ref=buffer.at[g, p],
            dst_ref=buffer.at[g, p],
            send_sem=sems.at[g, d - 1],
            recv_sem=sems.at[g, d - 1],
            device_id=at_peer(p),
            device_id_type=MESH,
        ).wait_recv()

    def dispatch(g):
        value = jnp.full((128, 128), -1.0, F32)
        for q in range(4):
            for c in range(2):
                line = met[4 * g + q, pl.ds(2 * z + c, 1), :]
                value = jnp.where((row_q == q) & (row_c == c), line, value)
        rank_here = (
            jnp.where(value >= 2.0, 1.0, 0.0)
            + jnp.where(value >= 4.0, 1.0, 0.0)
            + jnp.where(value >= 6.0, 1.0, 0.0)
        )
        picked = (value >= 0.0) & (lane_g == row_x) & (rank_here == row_s.astype(F32))
        choose = folded(jnp.where(picked, 1.0, 0.0)).astype(BF)
        weigh = folded(jnp.where(picked, value - 2.0 * rank_here, 0.0))
        swt[g] = weigh.T.astype(BF)
        for c in range(4):
            cols = slice(512 * c, 512 * c + 512)
            rows = tok[4 * g : 4 * g + 4, :, cols].reshape(128, 512)
            sent = jnp.dot(choose, rows, preferred_element_type=F32).astype(BF)
            sendx[g, :, :, cols] = sent.reshape(8, 16, 512)
        for d in range(1, 8):
            x_copy(g, d).start()
        rx[g, me8] = sendx[g, me8]

    for k in range(1, 9):
        for half in range(2):
            for dr in range(2):
                if half == 0 and (dr, k) in met_copy:
                    met_copy[dr, k].wait_recv()
                    if (dr, k + 1) in met_copy:
                        met_copy[dr, k + 1].start()
                if (dr, k, half) in tok_copy:
                    tok_copy[dr, k, half].wait_recv()
                    if (dr, k + 1, half) in tok_copy:
                        tok_copy[dr, k + 1, half].start()
        if k % 2 == 0:
            dispatch(k // 2 - 1)
        if k in (2, 4, 6):
            for dr in range(2):
                w_copy[dr, k // 2 - 1, dr].wait_recv()
                v_copy[dr, k // 2 - 1].start()

    for g in range(4):
        for d in range(1, 8):
            landed(rx, x_r, g, d)

    def hidden_units(slot, rows):
        gate_pre = lax.dot_general(rows, wb[slot, 0:192], NT, preferred_element_type=F32)
        up_pre = lax.dot_general(rows, wb[slot, 192:384], NT, preferred_element_type=F32)
        return (gate_pre * (1.0 / (1.0 + jnp.exp(-gate_pre))) * up_pre).astype(BF)

    def quarter(slot):
        def body(h, carry):
            act = hidden_units(slot, rx[pl.ds(2 * h, 2)].reshape(256, D))
            for c in range(4):
                cols = slice(512 * c, 512 * c + 512)
                part_out = jnp.dot(act, wb[slot, 384:576, cols], preferred_element_type=F32)
                if slot == 0:
                    acc[pl.ds(2 * h, 2), :, cols] = part_out.reshape(2, 128, 512)
                else:
                    acc[pl.ds(2 * h, 2), :, cols] += part_out.reshape(2, 128, 512)
            return carry

        lax.fori_loop(0, 2, body, 0)

    quarter(0)
    for dr in range(2):
        for a in range(3):
            w_copy[dr, a, 1 - dr].wait_recv()
        quarter(1 + dr)
    for dr in range(2):
        for a in range(3):
            v_copy[dr, a].wait_recv()

    def last_quarter(g):
        act = hidden_units(3, rx[g].reshape(128, D))
        for c in range(4):
            cols = slice(512 * c, 512 * c + 512)
            part_out = jnp.dot(act, wb[3, 384:576, cols], preferred_element_type=F32)
            ysend[g, :, :, cols] = (acc[g, :, cols] + part_out).astype(BF).reshape(8, 16, 512)
        for d in range(1, 8):
            y_copy(g, d).start()
        ry[g, me8] = ysend[g, me8]

    for g in (3, 2, 1, 0):
        last_quarter(g)

    def gather_back(g):
        for d in range(1, 8):
            landed(ry, y_r, g, d)
        for c in range(4):
            cols = slice(512 * c, 512 * c + 512)
            rows = ry[g, :, :, cols].reshape(128, 512)
            mixed = jnp.dot(swt[g], rows, preferred_element_type=F32)
            part[4 * g : 4 * g + 4, :, cols] = mixed.reshape(4, 32, 512)

    rs_copy = {}
    for dr in range(2):
        for j in range(8):
            for half in range(2):
                if j == 0 and half != dr:
                    continue
                rows = pl.ds(16 * half, 16)
                rs_copy[dr, j, half] = pltpu.make_async_remote_copy(
                    src_ref=rss.at[dr, j, rows],
                    dst_ref=rsr.at[dr, j, rows],
                    send_sem=rs_s.at[dr, j, half],
                    recv_sem=rs_r.at[dr, j, half],
                    device_id=z_next[dr],
                    device_id_type=MESH,
                )

    gather_back(3)
    for j in range(8):
        distance = 8 - j
        if j in (2, 4, 6):
            gather_back(3 - j // 2)
        for half in range(2):
            rows = slice(16 * half, 16 * half + 16)
            for dr in range(2):
                if (dr, j, half) not in rs_copy:
                    continue
                source = slot_of(1 - dr, distance)
                total = part[source, rows, :]
                if (dr, j - 1, half) in rs_copy:
                    rs_copy[dr, j - 1, half].wait_recv()
                    total = total + rsr[dr, j - 1, rows, :].astype(F32)
                rss[dr, j, rows, :] = total.astype(BF)
                rs_copy[dr, j, half].start()
    for half in range(2):
        rows = slice(16 * half, 16 * half + 16)
        total = hid[rows, :] + part[0, rows, :]
        for dr in range(2):
            rs_copy[dr, 7, half].wait_recv()
            total = total + rsr[dr, 7, rows, :].astype(F32)
        out[rows, :] = total.astype(BF)

    for group in (tok_copy, met_copy, w_copy, v_copy, rs_copy):
        for copy in group.values():
            copy.wait_send()
    for copy in p_copy:
        copy.wait_send()
    for d in range(1, 4):
        for a in range(5):
            exchange(d, a).wait_send()
    for k in range(1, 9):
        for dr in range(2):
            if k < 8 or dr == 0:
                ring_row(dr, k).wait_send()
    for d in range(1, 8):
        router_rows(d, False).wait_send()
    for g in range(4):
        for d in range(1, 8):
            x_copy(g, d).wait_send()
            y_copy(g, d).wait_send()


def layer(*operands):
    vmem = pl.BlockSpec(memory_space=pltpu.VMEM)
    anywhere = pl.BlockSpec(memory_space=pl.ANY)
    dma = pltpu.SemaphoreType.DMA
    return pl.pallas_call(
        layer_kernel,
        out_shape=jax.ShapeDtypeStruct((TOK, D), BF),
        in_specs=[anywhere] * 5 + [vmem, anywhere] + [vmem] * 3 + [anywhere] * 3,
        out_specs=vmem,
        scratch_shapes=[
            pltpu.VMEM((4, TOK, 512), BF),
            pltpu.VMEM((4, 256, 128), BF),
            pltpu.VMEM((4, 256, 128), BF),
            pltpu.VMEM((4, TOK, 128), BF),
            pltpu.VMEM((4, TOK, 128), BF),
            pltpu.VMEM((4, TOK, 512), BF),
            pltpu.VMEM((512, D), BF),
            pltpu.VMEM((4, TOK, D), BF),
            pltpu.VMEM((3, TOK, D), BF),
            pltpu.VMEM((TOK, D), F32),
            pltpu.VMEM((4, ZN, 2, 16, 128), BF),
            pltpu.VMEM((2048, 128), F32),
            pltpu.VMEM((128, D), BF),
            pltpu.VMEM((16, TOK, D), BF),
            pltpu.VMEM((16, TOK, 128), F32),
            pltpu.VMEM((4, 128, 128), BF),
            pltpu.VMEM((4, 8, 16, D), BF),
            pltpu.VMEM((4, 8, 16, D), BF),
            pltpu.VMEM((4, 128, D), F32),
            pltpu.VMEM((4, 8, 16, D), BF),
            pltpu.VMEM((4, 8, 16, D), BF),
            pltpu.VMEM((16, TOK, D), F32),
            pltpu.VMEM((2, 8, TOK, D), BF),
            pltpu.VMEM((2, 8, TOK, D), BF),
            pltpu.VMEM((4, 576, D), BF),
            dma((3, 5)), dma((3, 5)), dma((6,)),
            dma((3,)), dma((3,)),
            dma((2, 8)), dma((2, 8)),
            dma((7,)), dma((7,)),
            dma((2, 8, 2)), dma((2, 8, 2)),
            dma((2, 8)), dma((2, 8)),
            dma((4, 7)), dma((4, 7)),
            dma((4, 7)), dma((4, 7)),
            dma((2, 8, 2)), dma((2, 8, 2)),
            dma((2, 3, 2)), dma((2, 3, 2)),
            dma((2, 3)), dma((2, 3)),
            dma((3,)),
        ],
        compiler_params=pltpu.CompilerParams(
            collective_id=0, has_side_effects=True, vmem_limit_bytes=56 * 1024 * 1024
        ),
        cost_estimate=pl.CostEstimate(
            flops=2 * 3 * 512 * 2048 * 768, bytes_accessed=8 << 20, transcendentals=512 * 768
        ),
    )(*operands)


def per_device(
    queries,
    block_keys,
    block_values,
    cache_keys,
    cache_values,
    residual,
    out_weight,
    norm_gain,
    router,
    gate_weight,
    up_weight,
    down_weight,
    expert_ids,
):
    block_output = layer(
        queries.reshape(TOK, D),
        block_keys.reshape(TOK, 256),
        block_values.reshape(TOK, 256),
        cache_keys.reshape(256, 256),
        cache_values.reshape(256, 256),
        residual.reshape(TOK, D),
        out_weight,
        norm_gain.reshape(1, D),
        router.reshape(16, 128),
        expert_ids.reshape(TOK, TOPK).T,
        gate_weight[0].T,
        up_weight[0].T,
        down_weight[0].T,
    )
    return block_output.reshape(residual.shape)


def solution(mesh):
    in_specs = (
        P("exp", "ctx", None, None),
        P("exp", "ctx", None, None),
        P("exp", "ctx", None, None),
        P("exp", "ctx", None),
        P("exp", "ctx", None),
        P("exp", "ctx", None, None),
        P("ctx", None),
        P(),
        P(None, "exp"),
        P("exp", None, "ctx"),
        P("exp", None, "ctx"),
        P("exp", None, "ctx"),
        P("exp", "ctx", None, None),
    )
    out_specs = P("exp", "ctx", None, None)
    return jax.shard_map(
        per_device, mesh=mesh, in_specs=in_specs, out_specs=out_specs, check_vma=False
    )
```

time: 455 us -> 161 us (0.35)
  waiting for transfers between devices: 271 us -> 0 us
  Pallas kernels: 0 us -> 149 us
  starting transfers between devices: 44.7 us -> 0 us
  matrix products: 37 us -> 0 us
  blocking collectives: 29.9 us -> 0 us
  local copies, waits for them, and re-layouts: 35.8 us -> 8.89 us
  other arithmetic: 21.6 us -> 1.32 us
  between operations: 13.5 us -> 0.01 us
    all_to_all x3 -> x0, waiting for transfers between devices: 194 us -> none  [the longest x1 98.2 us: per_device(): lax.all_to_all(outgoing, 'exp', split_axis=0, concat_axis=0, tiled=True)]
    pallas_call x0 -> x1, Pallas kernels: none -> 149 us  [layer(): pl.pallas_call(layer_kernel, out_shape=jax.ShapeDtypeStruct((TOK, D), BF)...]
    all_gather x4 -> x0, waiting for transfers between devices: 49.9 us -> none  [the longest x1 44.5 us: combined_all(): everything = jax.tree.map(lambda part: lax.all_gather(part, axis), shard)]
    all_to_all x3 -> x0, starting transfers between devices: 44.6 us -> none  [the longest x1 18.8 us: per_device(): lax.all_to_all(outgoing, 'exp', split_axis=0, concat_axis=0, tiled=True)]
    dot_general x15 -> x0, matrix products: 37 us -> none  [the longest x4 19.8 us: expert_part(): lax.dot_general(activated, down_piece, (((1,), (1,)), ((), ())), preferre...]
    all_gather x3 -> x0, blocking collectives: 29.9 us -> none  [the longest x2 18.4 us: combined_all(): everything = jax.tree.map(lambda part: lax.all_gather(part, axis), shard)]
    unnamed x6 -> x0, waiting for transfers between devices: 27.2 us -> none
    reshape x11 -> x6, local copies, waits for them, and re-layouts: 20.2 us -> 8.89 us  [the longest x1 1.66 us: per_device(): return block_output.reshape(residual.shape)]
  transfers between devices with their start and end apart: 8 -> 0, of which waited for: 5 -> 0; matrix products, arithmetic and copies ran while one was open for 13% -> 0% of each run, Pallas kernels for 0% -> 0%
where the time goes in v1:
time: 161 us; the launch traced here: 159 us
  Pallas kernels  149 us (93%)
  local copies, waits for them, and re-layouts  8.89 us (6%)
    pallas_call x1, Pallas kernels, layer(): pl.pallas_call(layer_kernel, out_shape=jax.ShapeDtypeStruct((TOK, D), BF)...  149 us

profile of v1, /device:TPU:1, one launch (start us, length us, event | category | flops | bytes accessed | tf_op | source)
XLA Modules:
  0.0 158.7 jit_solution(12202926683516051452)
XLA Ops:
  0.0 1.3 reduce
  1.3 1.4 copy.15
  2.7 1.3 reshape.31.block_keys
  4.0 1.3 reshape.32.block_values
  5.3 1.6 %reshape.30.queries = bf16[32,2048]{1,0:T(8,128)(2,1)} reshape(bf16[2,8,2,2048]{3,2,1,0:T(2,128)(2,1)} %param.13) | data formatting | bytes 262144 | tf_op jit(solution)/shard_map/reshape | solution.py:600
  7.0 1.6 %reshape.35.residual = bf16[32,2048]{1,0:T(8,128)(2,1)} reshape(bf16[2,8,2,2048]{3,2,1,0:T(2,128)(2,1)} %param.18) | data formatting | bytes 262144 | tf_op jit(solution)/shard_map/reshape | solution.py:605
  8.5 148.5 %shard_map.127 = bf16[32,2048]{1,0:T(8,128)(2,1)} custom-call(bf16[32,2048]{1,0:T(8,128)(2,1)} %reshape.30.queries, bf16[32,256]{1,0:T(8,128)(2,1)} %reshape.31.block_keys, bf16[32,256]{1,0:T(8,128)(2,1)} %reshape.32.block_values, bf16[256,256]{1,0:T(8,128)(2,1)} %bitcast.21, bf16[256,256]{1,0:T(8,128)(2,1)} %bitcast.22, bf16[32,2048]{1,0:T(8,128)(2,1)} %reshape.35.residual, ...), custom_call_target="tpu_custom_call" | custom-call | flops 4831838208 | bytes 8388608 | tf_op jit(solution)/shard_map/pallas_call | solution.py:531
  157.1 1.7 %reshape.39 = bf16[2,8,2,2048]{3,2,1,0:T(2,128)(2,1)} reshape(bf16[32,2048]{1,0:T(8,128)(2,1)} %shard_map.127) | data formatting | bytes 262144 | tf_op jit(solution)/shard_map/reshape | solution.py:614

commit v2 on v1

v2 whole, which is shorter than its diff:
```python
import functools

import jax
import jax.numpy as jnp
from jax import lax
from jax.experimental import pallas as pl
from jax.experimental.pallas import tpu as pltpu
from jax.sharding import PartitionSpec as P

D = 2048
HEAD_DIM = 128
TOPK = 8


MESH = pl.DeviceIdType.MESH
BF = jnp.bfloat16
F32 = jnp.float32
NT = (((1,), (1,)), ((), ()))
TOK = 32
ZN = 16


def slot_of(direction, distance):
    if distance == 8:
        return 15
    return 2 * distance - 1 + direction


def layer_kernel(
    q_in, bk_in, bv_in, cache_keys, cache_values, residual, out_weight,
    gain, router, ids, gate, up, down, out,
    queries, block_keys, block_values, q_all, k_all, v_all, bk_all, bv_all, att, ow, psend, precv, hid, rt, rg, rgf, rfull,
    tok, met, swt, sendx, rx, act, ysend, ry, part, rss, rsr, wb,
    ex_s, ex_r, own_l, p_s, p_r, rz_s, rz_r, rp_s, rp_r,
    tok_s, tok_r, met_s, met_r, x_s, x_r, y_s, y_r, rs_s, rs_r,
    w_s, w_r, v_s, v_r, o_s, o_r, loc,
):
    y = lax.axis_index("ctx")
    e = lax.axis_index("exp")
    core = lax.rem(e, 2)
    z = lax.rem(e // 2, ZN)
    x = e // 32
    me8 = x * 2 + core

    def at_z(other):
        return (y, x * 32 + other * 2 + core)

    def at_peer(p):
        return (y, (p // 2) * 32 + z * 2 + lax.rem(p, 2))

    def at_slot(p):
        kept = lax.rem(p, 2)
        return (lax.rem(y + kept * (1 + 2 * core), 4), (p // 2) * 32 + z * 2 + kept)

    def at_source(p):
        other = lax.rem(p, 2)
        return (lax.rem(y + core * (3 - 2 * other), 4), (p // 2) * 32 + z * 2 + other)

    def at_line(d, c):
        return (lax.rem(y + d, 4), x * 32 + z * 2 + c)

    def at_y(d):
        return at_line(d, core)

    def at_across(d, k, c):
        return (lax.rem(y + d, 4), lax.rem(x + k, 4) * 32 + z * 2 + c)

    z_next = (at_z(lax.rem(z + 1, ZN)), at_z(lax.rem(z + ZN - 1, ZN)))
    sibling = at_line(0, 1 - core)
    keeper = core == lax.rem(y, 2)

    pending = []

    def go(copy):
        copy.start()
        pending.append(copy)
        return copy

    barrier = pltpu.get_barrier_semaphore()

    def greet(target):
        pl.semaphore_signal(barrier, inc=1, device_id=target, device_id_type=MESH)

    for d in range(1, ZN):
        greet(at_z(lax.rem(z + d, ZN)))
    for d in range(1, 8):
        greet(at_peer(lax.rem(me8 + d, 8)))
    for d in range(1, 4):
        for c in range(2):
            greet(at_line(d, c))

    @pl.when(core == 0)
    def _():
        for k in range(1, 4):
            greet(at_across(1, k, 1))

    @pl.when(core == 1)
    def _():
        for k in range(1, 4):
            greet(at_across(3, k, 0))
            greet(at_across(3, k, 1))
            greet(at_across(1, k, 1))

    weights = (gate, up, down)
    own_copies = []

    def own_weight(a):
        return pltpu.make_async_copy(weights[a], wb.at[0, pl.ds(192 * a, 192)], loc.at[a])

    @pl.when(keeper)
    def _():
        for a in range(3):
            own_weight(a).start()

    queries[...] = q_in[...].reshape(TOK, D)
    block_keys[...] = bk_in[...].reshape(TOK, 256)
    block_values[...] = bv_in[...].reshape(TOK, 256)
    for k in range(16):
        rt[k : k + 1, :] = router[0:1, 128 * k : 128 * k + 128].astype(F32)
    rg[x, z, core] = rt[...].astype(BF)

    def columns(index, width):
        return pl.ds(pl.multiple_of(index * width, width), width)

    def shares(owner):
        group = owner // 2
        return (
            queries.at[:, columns(owner, 512)],
            cache_keys.at[:, columns(group, 128)],
            cache_values.at[:, columns(group, 128)],
            block_keys.at[:, columns(group, 128)],
            block_values.at[:, columns(group, 128)],
        )

    gathered = (q_all, k_all, v_all, bk_all, bv_all)
    for a, share in enumerate(shares(y)):
        copy = pltpu.make_async_copy(share, gathered[a].at[y], own_l.at[a])
        copy.start()
        own_copies.append(copy)
    copy = pltpu.make_async_copy(out_weight, ow, own_l.at[5])
    copy.start()
    own_copies.append(copy)

    pl.semaphore_wait(barrier, 31 + 6 * core)

    def exchange(d, a):
        owner = lax.rem(y + d, 4)
        return pltpu.make_async_remote_copy(
            src_ref=shares(owner)[a],
            dst_ref=gathered[a].at[y],
            send_sem=ex_s.at[d - 1, a],
            recv_sem=ex_r.at[d - 1, a],
            device_id=at_y(d),
            device_id_type=MESH,
        )

    def exchanged(d, a):
        source = lax.rem(y + 4 - d, 4)
        pltpu.make_async_remote_copy(
            src_ref=gathered[a].at[source],
            dst_ref=gathered[a].at[source],
            send_sem=ex_s.at[d - 1, a],
            recv_sem=ex_r.at[d - 1, a],
            device_id=at_y(d),
            device_id_type=MESH,
        ).wait_recv()

    for d in (2, 1, 3):
        for a in range(5):
            go(exchange(d, a))

    def router_row(d, landed_here):
        held = lax.rem(z + ZN - d, ZN) if landed_here else z
        return pltpu.make_async_remote_copy(
            src_ref=rg.at[x, held, core],
            dst_ref=rg.at[x, held, core],
            send_sem=rz_s.at[d - 1],
            recv_sem=rz_r.at[d - 1],
            device_id=at_z(lax.rem(z + d, ZN)),
            device_id_type=MESH,
        )

    def router_rows(d, landed_here):
        p = lax.rem(me8 + 8 - d, 8) if landed_here else me8
        return pltpu.make_async_remote_copy(
            src_ref=rg.at[p // 2, :, lax.rem(p, 2)],
            dst_ref=rg.at[p // 2, :, lax.rem(p, 2)],
            send_sem=rp_s.at[d - 1],
            recv_sem=rp_r.at[d - 1],
            device_id=at_peer(lax.rem(me8 + d, 8)),
            device_id_type=MESH,
        )

    pieces = ((0, 32), (32, 64))

    def give(dr, a, half, piece):
        start, count = pieces[piece]
        rows = pl.ds(192 * a + 96 * half + start, count)
        return pltpu.make_async_remote_copy(
            src_ref=weights[a].at[pl.ds(96 * half + start, count)],
            dst_ref=wb.at[1 + dr, rows],
            send_sem=w_s.at[dr, a, half, piece],
            recv_sem=w_r.at[dr, a, piece],
            device_id=at_line((1, 3, 2)[dr], half),
            device_id_type=MESH,
        )

    def share_weight(a):
        return pltpu.make_async_remote_copy(
            src_ref=weights[a],
            dst_ref=wb.at[0, pl.ds(192 * a, 192)],
            send_sem=o_s.at[a],
            recv_sem=o_r.at[a],
            device_id=sibling,
            device_id_type=MESH,
        )

    def send_weights(a, piece):
        @pl.when(keeper)
        def _():
            for half in range(2):
                give(2, a, half, piece).start()
            if piece == 1:
                share_weight(a).start()

        @pl.when(jnp.logical_not(keeper))
        def _():
            for half in range(2):
                give(0, a, half, piece).start()
                give(1, a, half, piece).start()

    def given(slot, a, piece):
        start, count = pieces[piece]
        rows = pl.ds(pl.multiple_of(192 * a + 96 * core + start, 32), count)
        pltpu.make_async_remote_copy(
            src_ref=wb.at[slot, rows],
            dst_ref=wb.at[slot, rows],
            send_sem=v_s.at[slot - 1, a],
            recv_sem=w_r.at[slot - 1, a, piece],
            device_id=sibling,
            device_id_type=MESH,
        ).wait_recv()

    def half_copy(slot, a, half):
        rows = pl.ds(pl.multiple_of(192 * a + 96 * half, 32), 96)
        return pltpu.make_async_remote_copy(
            src_ref=wb.at[slot, rows],
            dst_ref=wb.at[slot, rows],
            send_sem=v_s.at[slot - 1, a],
            recv_sem=v_r.at[slot - 1, a],
            device_id=sibling,
            device_id_type=MESH,
        )

    def pass_on(a):
        for slot in range(1, 4):
            for piece in range(2):
                given(slot, a, piece)
            go(half_copy(slot, a, core))

    def weight_ready(a):
        for slot in range(1, 4):
            half_copy(slot, a, 1 - core).wait_recv()

        @pl.when(keeper)
        def _():
            own_weight(a).wait()

        @pl.when(jnp.logical_not(keeper))
        def _():
            share_weight(a).wait_recv()

    for d in range(1, ZN):
        go(router_row(d, False))
    send_weights(0, 0)
    for d in range(1, ZN):
        router_row(d, True).wait_recv()
    for d in range(1, 8):
        go(router_rows(d, False))

    for copy in own_copies:
        copy.wait()
    for d in range(1, 4):
        for a in range(5):
            exchanged(d, a)

    key_step = lax.rem(lax.broadcasted_iota(jnp.int32, (256, 64), 1), 2)
    row_step = lax.rem(lax.broadcasted_iota(jnp.int32, (256, 64), 0), 2)
    for r in range(2):
        near, far = slice(16 * r, 16 * r + 16), slice(128 * r, 128 * r + 128)
        q_rows = jnp.concatenate(
            [q_all[m, near, 128 * h : 128 * h + 128] for h in range(4) for m in range(4)], 0
        )
        far_scores = lax.dot_general(
            q_rows, k_all[:, far, :].reshape(512, 128), NT, preferred_element_type=F32
        )
        near_scores = lax.dot_general(
            q_rows, bk_all[:, near, :].reshape(64, 128), NT, preferred_element_type=F32
        )
        far_scores = far_scores * HEAD_DIM ** (-0.5)
        near_scores = jnp.where(
            key_step == row_step, near_scores * HEAD_DIM ** (-0.5), -3e38
        )
        row_top = jnp.maximum(
            jnp.max(far_scores, -1, keepdims=True), jnp.max(near_scores, -1, keepdims=True)
        )
        far_exp = jnp.exp(far_scores - row_top)
        near_exp = jnp.where(key_step == row_step, jnp.exp(near_scores - row_top), 0.0)
        total = jnp.sum(far_exp, -1, keepdims=True) + jnp.sum(near_exp, -1, keepdims=True)
        weighted = jnp.dot(
            far_exp.astype(BF), v_all[:, far, :].reshape(512, 128), preferred_element_type=F32
        ) + jnp.dot(
            near_exp.astype(BF), bv_all[:, near, :].reshape(64, 128), preferred_element_type=F32
        )
        attended = (weighted / total).astype(BF)
        for h in range(4):
            for m in range(4):
                att[m, near, 128 * h : 128 * h + 128] = attended[
                    64 * h + 16 * m : 64 * h + 16 * m + 16
                ]

    for c in range(4):
        cols = slice(512 * c, 512 * c + 512)
        projected = jnp.dot(
            att[...].reshape(128, 512), ow[:, cols], preferred_element_type=F32
        ).reshape(4, TOK, 512)
        part[0:4, :, cols] = projected
        psend[:, :, cols] = projected.astype(BF)

    p_copy = []
    for d in (2, 1, 3):
        p_copy.append(
            pltpu.make_async_remote_copy(
                src_ref=psend.at[lax.rem(y + d, 4)],
                dst_ref=precv.at[d - 1],
                send_sem=p_s.at[d - 1],
                recv_sem=p_r.at[d - 1],
                device_id=at_y(d),
                device_id_type=MESH,
            )
        )
        go(p_copy[-1])
    send_weights(0, 1)
    send_weights(1, 0)
    send_weights(1, 1)

    for d in range(1, 8):
        router_rows(d, True).wait_recv()
    rgf[...] = rg[...].reshape(2048, 128).astype(F32)
    for k in range(16):
        rfull[:, 128 * k : 128 * k + 128] = rgf[pl.ds(k, 128, stride=16), :].astype(BF)

    for copy in p_copy:
        copy.wait_recv()
    hidden = residual[...].reshape(TOK, D).astype(F32) + part[y]
    for d in range(3):
        hidden = hidden + precv[d].astype(F32)
    hid[...] = hidden
    scale = lax.rsqrt(jnp.mean(hidden * hidden, -1, keepdims=True) + 1e-06)
    normed = (hidden * scale * gain[...]).astype(BF)
    tok[0] = normed
    scores = lax.dot_general(rfull[...], normed, NT, preferred_element_type=F32)
    scores = scores.astype(BF).astype(F32)
    id_rows = ids[...].reshape(TOK, TOPK)
    expert_lane = lax.broadcasted_iota(jnp.int32, (TOK, 128), 1)
    named = expert_lane == id_rows[:, 0:1]
    for k in range(1, TOPK):
        named = named | (expert_lane == id_rows[:, k : k + 1])
    hits = jnp.where(named, 1.0, 0.0).T
    named = hits > 0.0
    top = jnp.max(jnp.where(named, scores, -3e38), 0, keepdims=True)
    grown = jnp.where(named, jnp.exp(jnp.minimum(scores - top, 0.0)), 0.0)
    mix = grown / jnp.sum(grown, 0, keepdims=True)
    before = lax.broadcasted_iota(jnp.int32, (TOK, TOK), 0) < lax.broadcasted_iota(
        jnp.int32, (TOK, TOK), 1
    )
    rank = jnp.dot(
        hits.astype(BF), jnp.where(before, 1.0, 0.0).astype(BF), preferred_element_type=F32
    )
    code = jnp.where(named, 2.0 * rank + mix, -1.0)
    for k in range(4):
        met[0, :, 32 * k : 32 * k + 32] = code[32 * k : 32 * k + 32, :]

    tok_copy, met_copy = {}, {}
    for dr in range(2):
        for k in range(1, 9):
            src = 0 if k == 1 else slot_of(dr, k - 1)
            dst = slot_of(dr, k)
            for chunk in range(4):
                if k == 8 and chunk // 2 != dr:
                    continue
                rows, cols = pl.ds(16 * (chunk // 2), 16), pl.ds(1024 * (chunk % 2), 1024)
                tok_copy[dr, k, chunk] = pltpu.make_async_remote_copy(
                    src_ref=tok.at[src, rows, cols],
                    dst_ref=tok.at[dst, rows, cols],
                    send_sem=tok_s.at[dr, k - 1, chunk],
                    recv_sem=tok_r.at[dr, k - 1, chunk],
                    device_id=z_next[dr],
                    device_id_type=MESH,
                )
            if k < 8 or dr == 0:
                met_copy[dr, k] = pltpu.make_async_remote_copy(
                    src_ref=met.at[src],
                    dst_ref=met.at[dst],
                    send_sem=met_s.at[dr, k - 1],
                    recv_sem=met_r.at[dr, k - 1],
                    device_id=z_next[dr],
                    device_id_type=MESH,
                )

    for dr in range(2):
        go(met_copy[dr, 1])
    for chunk in range(4):
        for dr in range(2):
            go(tok_copy[dr, 1, chunk])
    pass_on(0)

    row = lax.broadcasted_iota(jnp.int32, (128, 128), 0)
    lane = lax.broadcasted_iota(jnp.int32, (128, 128), 1)
    row_x, row_c = row // 32, lax.rem(row // 16, 2)
    row_q, row_s = lax.rem(row // 4, 4), lax.rem(row, 4)
    lane_g = lane // 32

    def folded(values):
        total = values
        for k in range(1, 4):
            total = total + pltpu.roll(values, 32 * k, 1)
        return jnp.where(lane_g == row_q, total, 0.0)

    def x_copy(g, d):
        p = lax.rem(me8 + d, 8)
        return pltpu.make_async_remote_copy(
            src_ref=sendx.at[g, p],
            dst_ref=rx.at[g, me8],
            send_sem=x_s.at[g, d],
            recv_sem=x_r.at[g, d],
            device_id=at_slot(p),
            device_id_type=MESH,
        )

    def y_copy(g, d):
        p = lax.rem(me8 + d, 8)
        return pltpu.make_async_remote_copy(
            src_ref=ysend.at[g, p],
            dst_ref=ry.at[g, me8],
            send_sem=y_s.at[g, d],
            recv_sem=y_r.at[g, d],
            device_id=at_source(p),
            device_id_type=MESH,
        )

    def landed(buffer, sems, g, d):
        p = lax.rem(me8 + 8 - d, 8)
        pltpu.make_async_remote_copy(
            src_ref=buffer.at[g, p],
            dst_ref=buffer.at[g, p],
            send_sem=sems.at[g, d],
            recv_sem=sems.at[g, d],
            device_id=at_slot(p),
            device_id_type=MESH,
        ).wait_recv()

    def landed_all(buffer, sems, g):
        for d in range(1, 8):
            landed(buffer, sems, g, d)

        @pl.when(core == 1)
        def _():
            landed(buffer, sems, g, 0)

    def dispatch(g):
        held = {}

        def select():
            value = jnp.full((128, 128), -1.0, F32)
            for q in range(4):
                for c in range(2):
                    line = met[4 * g + q, pl.ds(2 * z + lax.rem(y + c, 2), 1), :]
                    value = jnp.where((row_q == q) & (row_c == c), line, value)
            rank_here = (
                jnp.where(value >= 2.0, 1.0, 0.0)
                + jnp.where(value >= 4.0, 1.0, 0.0)
                + jnp.where(value >= 6.0, 1.0, 0.0)
            )
            picked = (value >= 0.0) & (lane_g == row_x) & (rank_here == row_s.astype(F32))
            held["choose"] = folded(jnp.where(picked, 1.0, 0.0)).astype(BF)
            weigh = folded(jnp.where(picked, value - 2.0 * rank_here, 0.0))
            swt[g] = weigh.T.astype(BF)

        def pick(c):
            cols = slice(512 * c, 512 * c + 512)
            rows = tok[4 * g : 4 * g + 4, :, cols].reshape(128, 512)
            sent = jnp.dot(held["choose"], rows, preferred_element_type=F32).astype(BF)
            sendx[g, :, :, cols] = sent.reshape(8, 16, 512)

        def send():
            for d in range(1, 8):
                go(x_copy(g, d))

            @pl.when(core == 1)
            def _():
                x_copy(g, 0).start()

            @pl.when(core == 0)
            def _():
                rx[g, me8] = sendx[g, me8]

        return [select] + [functools.partial(pick, c) for c in range(4)] + [send]

    work = []

    def do_next():
        if work:
            work.pop(0)()

    def do_all():
        while work:
            do_next()

    for k in range(1, 9):
        for chunk in range(4):
            for dr in range(2):
                if chunk == 0 and (dr, k) in met_copy:
                    met_copy[dr, k].wait_recv()
                    if (dr, k + 1) in met_copy:
                        go(met_copy[dr, k + 1])
                if (dr, k, chunk) in tok_copy:
                    tok_copy[dr, k, chunk].wait_recv()
                    if (dr, k + 1, chunk) in tok_copy:
                        go(tok_copy[dr, k + 1, chunk])
            do_next()
        if k % 2 == 0:
            work.extend(dispatch(k // 2 - 1))
        if k == 2:
            work.append(functools.partial(send_weights, 2, 0))
            work.append(functools.partial(send_weights, 2, 1))
        if k == 6:
            work.append(functools.partial(pass_on, 1))
    do_all()

    for g in range(4):
        landed_all(rx, x_r, g)

    def hidden_units(slot):
        def body(h, carry):
            rows = rx[pl.ds(2 * h, 2)].reshape(256, D)
            gate_pre = lax.dot_general(rows, wb[slot, 0:192], NT, preferred_element_type=F32)
            up_pre = lax.dot_general(rows, wb[slot, 192:384], NT, preferred_element_type=F32)
            activated = gate_pre * (1.0 / (1.0 + jnp.exp(-gate_pre))) * up_pre
            act[slot, pl.ds(pl.multiple_of(256 * h, 256), 256), :] = activated.astype(BF)
            return carry

        lax.fori_loop(0, 2, body, 0)

    weight_ready(0)
    weight_ready(1)
    hidden_units(0)
    hidden_units(1)
    pass_on(2)
    hidden_units(2)
    hidden_units(3)
    weight_ready(2)

    def project(g):
        for c in range(4):
            cols = slice(512 * c, 512 * c + 512)
            total = jnp.dot(
                act[0, 128 * g : 128 * g + 128, :],
                wb[0, 384:576, cols],
                preferred_element_type=F32,
            )
            for slot in range(1, 4):
                total = total + jnp.dot(
                    act[slot, 128 * g : 128 * g + 128, :],
                    wb[slot, 384:576, cols],
                    preferred_element_type=F32,
                )
            ysend[g, :, :, cols] = total.astype(BF).reshape(8, 16, 512)
        for d in range(1, 8):
            go(y_copy(g, d))

        @pl.when(core == 1)
        def _():
            y_copy(g, 0).start()

        @pl.when(core == 0)
        def _():
            ry[g, me8] = ysend[g, me8]

    for g in (3, 2, 1, 0):
        project(g)

    def gather_back(g):
        def wait():
            landed_all(ry, y_r, g)

        def weigh(c):
            cols = slice(512 * c, 512 * c + 512)
            rows = ry[g, :, :, cols].reshape(128, 512)
            mixed = jnp.dot(swt[g], rows, preferred_element_type=F32)
            part[4 * g : 4 * g + 4, :, cols] = mixed.reshape(4, 32, 512)

        return [wait] + [functools.partial(weigh, c) for c in range(4)]

    rs_copy = {}
    for dr in range(2):
        for j in range(8):
            for chunk in range(4):
                if j == 0 and chunk // 2 != dr:
                    continue
                rows, cols = pl.ds(16 * (chunk // 2), 16), pl.ds(1024 * (chunk % 2), 1024)
                rs_copy[dr, j, chunk] = pltpu.make_async_remote_copy(
                    src_ref=rss.at[dr, j, rows, cols],
                    dst_ref=rsr.at[dr, j, rows, cols],
                    send_sem=rs_s.at[dr, j, chunk],
                    recv_sem=rs_r.at[dr, j, chunk],
                    device_id=z_next[dr],
                    device_id_type=MESH,
                )

    work.extend(gather_back(3))
    do_all()
    for j in range(8):
        if j in (2, 4, 6):
            do_all()
        if j in (1, 3, 5):
            work.extend([lambda: None] * 2 + gather_back(2 - j // 2))
        for chunk in range(4):
            rows = slice(16 * (chunk // 2), 16 * (chunk // 2) + 16)
            cols = slice(1024 * (chunk % 2), 1024 * (chunk % 2) + 1024)
            for dr in range(2):
                if (dr, j, chunk) not in rs_copy:
                    continue
                total = part[slot_of(1 - dr, 8 - j), rows, cols]
                if (dr, j - 1, chunk) in rs_copy:
                    rs_copy[dr, j - 1, chunk].wait_recv()
                    total = total + rsr[dr, j - 1, rows, cols].astype(F32)
                rss[dr, j, rows, cols] = total.astype(BF)
                go(rs_copy[dr, j, chunk])
            do_next()
    for chunk in range(4):
        rows = slice(16 * (chunk // 2), 16 * (chunk // 2) + 16)
        cols = slice(1024 * (chunk % 2), 1024 * (chunk % 2) + 1024)
        total = hid[rows, cols] + part[0, rows, cols]
        for dr in range(2):
            rs_copy[dr, 7, chunk].wait_recv()
            total = total + rsr[dr, 7, rows, cols].astype(F32)
        out[rows, cols] = total.astype(BF)

    for copy in pending:
        copy.wait_send()

    @pl.when(core == 1)
    def _():
        for g in range(4):
            x_copy(g, 0).wait_send()
            y_copy(g, 0).wait_send()

    @pl.when(keeper)
    def _():
        for a in range(3):
            for half in range(2):
                for piece in range(2):
                    give(2, a, half, piece).wait_send()
            share_weight(a).wait_send()

    @pl.when(jnp.logical_not(keeper))
    def _():
        for a in range(3):
            for half in range(2):
                for piece in range(2):
                    give(0, a, half, piece).wait_send()
                    give(1, a, half, piece).wait_send()


def layer(*operands):
    vmem = pl.BlockSpec(memory_space=pltpu.VMEM)
    anywhere = pl.BlockSpec(memory_space=pl.ANY)
    dma = pltpu.SemaphoreType.DMA
    return pl.pallas_call(
        layer_kernel,
        out_shape=jax.ShapeDtypeStruct((TOK, D), BF),
        in_specs=[vmem] * 3 + [anywhere] * 2 + [vmem, anywhere] + [vmem] * 3 + [anywhere] * 3,
        out_specs=vmem,
        scratch_shapes=[
            pltpu.VMEM((TOK, D), BF),
            pltpu.VMEM((TOK, 256), BF),
            pltpu.VMEM((TOK, 256), BF),
            pltpu.VMEM((4, TOK, 512), BF),
            pltpu.VMEM((4, 256, 128), BF),
            pltpu.VMEM((4, 256, 128), BF),
            pltpu.VMEM((4, TOK, 128), BF),
            pltpu.VMEM((4, TOK, 128), BF),
            pltpu.VMEM((4, TOK, 512), BF),
            pltpu.VMEM((512, D), BF),
            pltpu.VMEM((4, TOK, D), BF),
            pltpu.VMEM((3, TOK, D), BF),
            pltpu.VMEM((TOK, D), F32),
            pltpu.VMEM((16, 128), F32),
            pltpu.VMEM((4, ZN, 2, 16, 128), BF),
            pltpu.VMEM((2048, 128), F32),
            pltpu.VMEM((128, D), BF),
            pltpu.VMEM((16, TOK, D), BF),
            pltpu.VMEM((16, TOK, 128), F32),
            pltpu.VMEM((4, 128, 128), BF),
            pltpu.VMEM((4, 8, 16, D), BF),
            pltpu.VMEM((4, 8, 16, D), BF),
            pltpu.VMEM((4, 512, 192), BF),
            pltpu.VMEM((4, 8, 16, D), BF),
            pltpu.VMEM((4, 8, 16, D), BF),
            pltpu.VMEM((16, TOK, D), F32),
            pltpu.VMEM((2, 8, TOK, D), BF),
            pltpu.VMEM((2, 8, TOK, D), BF),
            pltpu.VMEM((4, 576, D), BF),
            dma((3, 5)), dma((3, 5)), dma((6,)),
            dma((3,)), dma((3,)),
            dma((15,)), dma((15,)),
            dma((7,)), dma((7,)),
            dma((2, 8, 4)), dma((2, 8, 4)),
            dma((2, 8)), dma((2, 8)),
            dma((4, 8)), dma((4, 8)),
            dma((4, 8)), dma((4, 8)),
            dma((2, 8, 4)), dma((2, 8, 4)),
            dma((3, 3, 2, 2)), dma((3, 3, 2)),
            dma((3, 3)), dma((3, 3)),
            dma((3,)), dma((3,)),
            dma((3,)),
        ],
        compiler_params=pltpu.CompilerParams(
            collective_id=0, has_side_effects=True, vmem_limit_bytes=56 * 1024 * 1024
        ),
        cost_estimate=pl.CostEstimate(
            flops=2 * 3 * 512 * 2048 * 768, bytes_accessed=8 << 20, transcendentals=512 * 768
        ),
    )(*operands)


def per_device(
    queries,
    block_keys,
    block_values,
    cache_keys,
    cache_values,
    residual,
    out_weight,
    norm_gain,
    router,
    gate_weight,
    up_weight,
    down_weight,
    expert_ids,
):
    block_output = layer(
        queries,
        block_keys,
        block_values,
        cache_keys.reshape(256, 256),
        cache_values.reshape(256, 256),
        residual,
        out_weight,
        norm_gain.reshape(1, D),
        router.T,
        expert_ids,
        gate_weight[0].T,
        up_weight[0].T,
        down_weight[0].T,
    )
    return block_output.reshape(residual.shape)


def solution(mesh):
    in_specs = (
        P("exp", "ctx", None, None),
        P("exp", "ctx", None, None),
        P("exp", "ctx", None, None),
        P("exp", "ctx", None),
        P("exp", "ctx", None),
        P("exp", "ctx", None, None),
        P("ctx", None),
        P(),
        P(None, "exp"),
        P("exp", None, "ctx"),
        P("exp", None, "ctx"),
        P("exp", None, "ctx"),
        P("exp", "ctx", None, None),
    )
    out_specs = P("exp", "ctx", None, None)
    return jax.shard_map(
        per_device, mesh=mesh, in_specs=in_specs, out_specs=out_specs, check_vma=False
    )
```

time: 161 us -> 146 us (0.907)
  local copies, waits for them, and re-layouts: 8.89 us -> 1.66 us
  Pallas kernels: 149 us -> 143 us
    reshape x5 -> x0, local copies, waits for them, and re-layouts: 7.23 us -> none  [the longest x1 1.61 us: per_device(): queries.reshape(TOK, D)]
    pallas_call x1, Pallas kernels: 149 us -> 143 us  [layer(): pl.pallas_call(layer_kernel, out_shape=jax.ShapeDtypeStruct((TOK, D), BF)...]
where the time goes in v2:
time: 146 us; the launch traced here: 144 us
  Pallas kernels  143 us (98%)
  local copies, waits for them, and re-layouts  1.66 us (1%)
    pallas_call x1, Pallas kernels, layer(): pl.pallas_call(layer_kernel, out_shape=jax.ShapeDtypeStruct((TOK, D), BF)...  143 us

profile of v2, /device:TPU:1, one launch (start us, length us, event | category | flops | bytes accessed | tf_op | source)
XLA Modules:
  0.0 144.3 jit_solution(12626325404714722462)
XLA Ops:
  0.0 142.6 %shard_map.127 = bf16[32,2048]{1,0:T(8,128)(2,1)} custom-call(bf16[2,8,2,2048]{3,2,1,0:T(2,128)(2,1)} %q_in.1, bf16[2,8,2,256]{3,2,1,0:T(2,128)(2,1)} %bk_in.1, bf16[2,8,2,256]{3,2,1,0:T(2,128)(2,1)} %bv_in.1, bf16[256,256]{1,0:T(8,128)(2,1)} %bitcast.16, bf16[256,256]{1,0:T(8,128)(2,1)} %bitcast.17, bf16[2,8,2,2048]{3,2,1,0:T(2,128)(2,1)} %residual.1, ...), custom_call_target="tpu_custom_call" | custom-call | flops 4831838208 | bytes 8388608 | tf_op jit(solution)/shard_map/pallas_call | solution.py:680
  142.6 1.7 %reshape.15 = bf16[2,8,2,2048]{3,2,1,0:T(2,128)(2,1)} reshape(bf16[32,2048]{1,0:T(8,128)(2,1)} %shard_map.127) | data formatting | bytes 262144 | tf_op jit(solution)/shard_map/reshape | solution.py:768

commit v3 on v2

--- a/solution.py
+++ b/solution.py
@@ -143,6 +143,20 @@
 
     pl.semaphore_wait(barrier, 31 + 6 * core)
 
+    def router_row(d, landed_here):
+        held = lax.rem(z + ZN - d, ZN) if landed_here else z
+        return pltpu.make_async_remote_copy(
+            src_ref=rg.at[x, held, core],
+            dst_ref=rg.at[x, held, core],
+            send_sem=rz_s.at[d - 1],
+            recv_sem=rz_r.at[d - 1],
+            device_id=at_z(lax.rem(z + d, ZN)),
+            device_id_type=MESH,
+        )
+
+    for d in range(1, ZN):
+        go(router_row(d, False))
+
     def exchange(d, a):
         owner = lax.rem(y + d, 4)
         return pltpu.make_async_remote_copy(
@@ -169,17 +183,6 @@
         for a in range(5):
             go(exchange(d, a))
 
-    def router_row(d, landed_here):
-        held = lax.rem(z + ZN - d, ZN) if landed_here else z
-        return pltpu.make_async_remote_copy(
-            src_ref=rg.at[x, held, core],
-            dst_ref=rg.at[x, held, core],
-            send_sem=rz_s.at[d - 1],
-            recv_sem=rz_r.at[d - 1],
-            device_id=at_z(lax.rem(z + d, ZN)),
-            device_id_type=MESH,
-        )
-
     def router_rows(d, landed_here):
         p = lax.rem(me8 + 8 - d, 8) if landed_here else me8
         return pltpu.make_async_remote_copy(
@@ -191,7 +194,7 @@
             device_id_type=MESH,
         )
 
-    pieces = ((0, 32), (32, 64))
+    pieces = ((0, 32), (32, 32), (64, 32))
 
     def give(dr, a, half, piece):
         start, count = pieces[piece]
@@ -220,7 +223,7 @@
         def _():
             for half in range(2):
                 give(2, a, half, piece).start()
-            if piece == 1:
+            if piece == 0:
                 share_weight(a).start()
 
         @pl.when(jnp.logical_not(keeper))
@@ -235,32 +238,38 @@
         pltpu.make_async_remote_copy(
             src_ref=wb.at[slot, rows],
             dst_ref=wb.at[slot, rows],
-            send_sem=v_s.at[slot - 1, a],
+            send_sem=v_s.at[slot - 1, a, piece],
             recv_sem=w_r.at[slot - 1, a, piece],
             device_id=sibling,
             device_id_type=MESH,
         ).wait_recv()
 
-    def half_copy(slot, a, half):
-        rows = pl.ds(pl.multiple_of(192 * a + 96 * half, 32), 96)
+    def half_copy(slot, a, half, start, count):
+        rows = pl.ds(pl.multiple_of(192 * a + 96 * half + start, 32), count)
         return pltpu.make_async_remote_copy(
             src_ref=wb.at[slot, rows],
             dst_ref=wb.at[slot, rows],
-            send_sem=v_s.at[slot - 1, a],
-            recv_sem=v_r.at[slot - 1, a],
+            send_sem=v_s.at[slot - 1, a, start // 32],
+            recv_sem=v_r.at[slot - 1, a, start // 32],
             device_id=sibling,
             device_id_type=MESH,
         )
 
     def pass_on(a):
         for slot in range(1, 4):
-            for piece in range(2):
+            for piece in range(3):
                 given(slot, a, piece)
-            go(half_copy(slot, a, core))
+            go(half_copy(slot, a, core, 0, 96))
+
+    def pass_piece(a, piece):
+        for slot in range(1, 4):
+            given(slot, a, piece)
+            go(half_copy(slot, a, core, *pieces[piece]))
 
     def weight_ready(a):
         for slot in range(1, 4):
-            half_copy(slot, a, 1 - core).wait_recv()
+            for start, count in pieces if a == 2 else ((0, 96),):
+                half_copy(slot, a, 1 - core, start, count).wait_recv()
 
         @pl.when(keeper)
         def _():
@@ -270,8 +279,6 @@
         def _():
             share_weight(a).wait_recv()
 
-    for d in range(1, ZN):
-        go(router_row(d, False))
     send_weights(0, 0)
     for d in range(1, ZN):
         router_row(d, True).wait_recv()
@@ -340,9 +347,8 @@
             )
         )
         go(p_copy[-1])
-    send_weights(0, 1)
-    send_weights(1, 0)
-    send_weights(1, 1)
+    for a, piece in ((0, 1), (0, 2), (1, 0), (1, 1), (1, 2)):
+        send_weights(a, piece)
 
     for d in range(1, 8):
         router_rows(d, True).wait_recv()
@@ -533,32 +539,34 @@
             work.extend(dispatch(k // 2 - 1))
         if k == 2:
             work.append(functools.partial(send_weights, 2, 0))
+        if k == 5:
             work.append(functools.partial(send_weights, 2, 1))
         if k == 6:
             work.append(functools.partial(pass_on, 1))
     do_all()
 
-    for g in range(4):
-        landed_all(rx, x_r, g)
-
-    def hidden_units(slot):
-        def body(h, carry):
-            rows = rx[pl.ds(2 * h, 2)].reshape(256, D)
-            gate_pre = lax.dot_general(rows, wb[slot, 0:192], NT, preferred_element_type=F32)
-            up_pre = lax.dot_general(rows, wb[slot, 192:384], NT, preferred_element_type=F32)
-            activated = gate_pre * (1.0 / (1.0 + jnp.exp(-gate_pre))) * up_pre
-            act[slot, pl.ds(pl.multiple_of(256 * h, 256), 256), :] = activated.astype(BF)
-            return carry
-
-        lax.fori_loop(0, 2, body, 0)
-
+    send_weights(2, 2)
+
+    def hidden_units(slot, h):
+        rows = rx[2 * h : 2 * h + 2].reshape(256, D)
+        gate_pre = lax.dot_general(rows, wb[slot, 0:192], NT, preferred_element_type=F32)
+        up_pre = lax.dot_general(rows, wb[slot, 192:384], NT, preferred_element_type=F32)
+        activated = gate_pre * (1.0 / (1.0 + jnp.exp(-gate_pre))) * up_pre
+        act[slot, 256 * h : 256 * h + 256, :] = activated.astype(BF)
+
+    landed_all(rx, x_r, 0)
+    landed_all(rx, x_r, 1)
     weight_ready(0)
     weight_ready(1)
-    hidden_units(0)
-    hidden_units(1)
-    pass_on(2)
-    hidden_units(2)
-    hidden_units(3)
+    for slot in range(4):
+        hidden_units(slot, 0)
+    pass_piece(2, 0)
+    pass_piece(2, 1)
+    landed_all(rx, x_r, 2)
+    landed_all(rx, x_r, 3)
+    for slot in range(4):
+        hidden_units(slot, 1)
+    pass_piece(2, 2)
     weight_ready(2)
 
     def project(g):
@@ -660,7 +668,7 @@
     def _():
         for a in range(3):
             for half in range(2):
-                for piece in range(2):
+                for piece in range(3):
                     give(2, a, half, piece).wait_send()
             share_weight(a).wait_send()
 
@@ -668,7 +676,7 @@
     def _():
         for a in range(3):
             for half in range(2):
-                for piece in range(2):
+                for piece in range(3):
                     give(0, a, half, piece).wait_send()
                     give(1, a, half, piece).wait_send()
 
@@ -721,8 +729,8 @@
             dma((4, 8)), dma((4, 8)),
             dma((4, 8)), dma((4, 8)),
             dma((2, 8, 4)), dma((2, 8, 4)),
-            dma((3, 3, 2, 2)), dma((3, 3, 2)),
-            dma((3, 3)), dma((3, 3)),
+            dma((3, 3, 2, 3)), dma((3, 3, 3)),
+            dma((3, 3, 3)), dma((3, 3, 3)),
             dma((3,)), dma((3,)),
             dma((3,)),
         ],

time: 146 us -> 142 us (0.973)
  Pallas kernels: 143 us -> 139 us
    pallas_call x1, Pallas kernels: 143 us -> 139 us  [layer(): pl.pallas_call(layer_kernel, out_shape=jax.ShapeDtypeStruct((TOK, D), BF)...]
where the time goes in v3:
time: 142 us; the launch traced here: 141 us
  Pallas kernels  139 us (98%)
  local copies, waits for them, and re-layouts  1.66 us (1%)
    pallas_call x1, Pallas kernels, layer(): pl.pallas_call(layer_kernel, out_shape=jax.ShapeDtypeStruct((TOK, D), BF)...  139 us

profile of v3, /device:TPU:1, one launch (start us, length us, event | category | flops | bytes accessed | tf_op | source)
XLA Modules:
  0.0 140.9 jit_solution(15118770639342149592)
XLA Ops:
  0.0 139.2 %shard_map.127 = bf16[32,2048]{1,0:T(8,128)(2,1)} custom-call(bf16[2,8,2,2048]{3,2,1,0:T(2,128)(2,1)} %q_in.1, bf16[2,8,2,256]{3,2,1,0:T(2,128)(2,1)} %bk_in.1, bf16[2,8,2,256]{3,2,1,0:T(2,128)(2,1)} %bv_in.1, bf16[256,256]{1,0:T(8,128)(2,1)} %bitcast.16, bf16[256,256]{1,0:T(8,128)(2,1)} %bitcast.17, bf16[2,8,2,2048]{3,2,1,0:T(2,128)(2,1)} %residual.1, ...), custom_call_target="tpu_custom_call" | custom-call | flops 4831838208 | bytes 8388608 | tf_op jit(solution)/shard_map/pallas_call | solution.py:688
  139.2 1.7 %reshape.15 = bf16[2,8,2,2048]{3,2,1,0:T(2,128)(2,1)} reshape(bf16[32,2048]{1,0:T(8,128)(2,1)} %shard_map.127) | data formatting | bytes 262144 | tf_op jit(solution)/shard_map/reshape | solution.py:776

commit v4 on v3

--- a/solution.py
+++ b/solution.py
@@ -27,9 +27,9 @@
 
 
 def layer_kernel(
-    q_in, bk_in, bv_in, cache_keys, cache_values, residual, out_weight,
+    q_in, bk_in, bv_in, cache_keys, cache_values, res_in, out_weight,
     gain, router, ids, gate, up, down, out,
-    queries, block_keys, block_values, q_all, k_all, v_all, bk_all, bv_all, att, ow, psend, precv, hid, rt, rg, rgf, rfull,
+    residual, queries, block_keys, block_values, q_all, k_all, v_all, bk_all, bv_all, att, ow, psend, precv, hid, rt, rg, rgf, rfull,
     tok, met, swt, sendx, rx, act, ysend, ry, part, rss, rsr, wb,
     ex_s, ex_r, own_l, p_s, p_r, rz_s, rz_r, rp_s, rp_r,
     tok_s, tok_r, met_s, met_r, x_s, x_r, y_s, y_r, rs_s, rs_r,
@@ -137,6 +137,9 @@
         copy = pltpu.make_async_copy(share, gathered[a].at[y], own_l.at[a])
         copy.start()
         own_copies.append(copy)
+    copy = pltpu.make_async_copy(res_in, residual, own_l.at[6])
+    copy.start()
+    own_copies.append(copy)
     copy = pltpu.make_async_copy(out_weight, ow, own_l.at[5])
     copy.start()
     own_copies.append(copy)
@@ -280,6 +283,7 @@
             share_weight(a).wait_recv()
 
     send_weights(0, 0)
+    send_weights(0, 1)
     for d in range(1, ZN):
         router_row(d, True).wait_recv()
     for d in range(1, 8):
@@ -347,7 +351,7 @@
             )
         )
         go(p_copy[-1])
-    for a, piece in ((0, 1), (0, 2), (1, 0), (1, 1), (1, 2)):
+    for a, piece in ((0, 2), (1, 0), (1, 1), (1, 2)):
         send_weights(a, piece)
 
     for d in range(1, 8):
@@ -688,9 +692,10 @@
     return pl.pallas_call(
         layer_kernel,
         out_shape=jax.ShapeDtypeStruct((TOK, D), BF),
-        in_specs=[vmem] * 3 + [anywhere] * 2 + [vmem, anywhere] + [vmem] * 3 + [anywhere] * 3,
+        in_specs=[vmem] * 3 + [anywhere] * 4 + [vmem] * 3 + [anywhere] * 3,
         out_specs=vmem,
         scratch_shapes=[
+            pltpu.VMEM((2, 8, 2, D), BF),
             pltpu.VMEM((TOK, D), BF),
             pltpu.VMEM((TOK, 256), BF),
             pltpu.VMEM((TOK, 256), BF),
@@ -720,7 +725,7 @@
             pltpu.VMEM((2, 8, TOK, D), BF),
             pltpu.VMEM((2, 8, TOK, D), BF),
             pltpu.VMEM((4, 576, D), BF),
-            dma((3, 5)), dma((3, 5)), dma((6,)),
+            dma((3, 5)), dma((3, 5)), dma((7,)),
             dma((3,)), dma((3,)),
             dma((15,)), dma((15,)),
             dma((7,)), dma((7,)),

time: 142 us -> 142 us (level)
  no operation moved by 1% of the time
where the time goes in v4:
time: 142 us; the launch traced here: 141 us
  Pallas kernels  139 us (98%)
  local copies, waits for them, and re-layouts  1.66 us (1%)
    pallas_call x1, Pallas kernels, layer(): pl.pallas_call(layer_kernel, out_shape=jax.ShapeDtypeStruct((TOK, D), BF)...  139 us

profile of v4, /device:TPU:1, one launch (start us, length us, event | category | flops | bytes accessed | tf_op | source)
XLA Modules:
  0.0 140.6 jit_solution(17690817711241390920)
XLA Ops:
  0.0 138.9 %shard_map.127 = bf16[32,2048]{1,0:T(8,128)(2,1)} custom-call(bf16[2,8,2,2048]{3,2,1,0:T(2,128)(2,1)} %q_in.1, bf16[2,8,2,256]{3,2,1,0:T(2,128)(2,1)} %bk_in.1, bf16[2,8,2,256]{3,2,1,0:T(2,128)(2,1)} %bv_in.1, bf16[256,256]{1,0:T(8,128)(2,1)} %bitcast.16, bf16[256,256]{1,0:T(8,128)(2,1)} %bitcast.17, bf16[2,8,2,2048]{3,2,1,0:T(2,128)(2,1)} %res_in.1, ...), custom_call_target="tpu_custom_call" | custom-call | flops 4831838208 | bytes 8388608 | tf_op jit(solution)/shard_map/pallas_call | solution.py:692
  138.9 1.7 %reshape.15 = bf16[2,8,2,2048]{3,2,1,0:T(2,128)(2,1)} reshape(bf16[32,2048]{1,0:T(8,128)(2,1)} %shard_map.127) | data formatting | bytes 262144 | tf_op jit(solution)/shard_map/reshape | solution.py:781
